TPU v7x, 32 devices: a whole 2x2x4 slice. The times are simulated.
32 devices in a mesh: section: 2 (over core), ctx: 4 (over y, x), tp: 4 (over z).
Axes of the slice: x: 2, y: 2, z: 4, core: 2. Of those that a mesh axis runs over, the one named last changes fastest.
Arguments:
- layer_inputs: bfloat16 [2, 6, 2, 1024, 1024], P('section', None, None, ('ctx', 'tp')), may hold values from -6 to 6
- out_grad: bfloat16 [6, 2, 1024, 1024], P(None, None, ('ctx', 'tp')), may hold values from -6 to 6
- src_seg: int32 [6, 2, 1024], P(None, None, 'ctx'), may hold values from 0 to 3, as said below
- tgt_seg: int32 [6, 2, 1024], P(None, None, 'ctx'), may hold values from 0 to 3, as said below
- qkv_weights: bfloat16 [2, 3, 1024, 1024], P('section', None, None, 'tp'), may hold values from -0.1875 to 0.1875
- out_weights: bfloat16 [2, 1024, 1024], P('section', None, 'tp'), may hold values from -0.75 to 0.75
- cross_weights: bfloat16 [2, 2, 1024, 1024], P('section', None, None, 'tp'), may hold values from -0.5 to 0.5, as said below
- ffn_in: bfloat16 [2, 1024, 4096], P('section', None, 'tp'), may hold values from -0.1875 to 0.1875
- ffn_out: bfloat16 [2, 4096, 1024], P('section', 'tp'), may hold values from -0.09375 to 0.09375
- adapter_in: bfloat16 [2, 1024, 512], P('section', None, 'tp'), may hold values from -0.1875 to 0.1875
- adapter_in_bias: bfloat16 [2, 512], P('section', 'tp'), may hold values from -4 to 4
- adapter_out: bfloat16 [2, 512, 1024], P('section', 'tp'), may hold values from -0.0625 to 0.0625
- adapter_out_bias: bfloat16 [2, 1024], P('section'), may hold values from -0.875 to 0.875
Outputs:
- layer_outputs: bfloat16 [2, 6, 2, 1024, 1024], P('section', None, None, ('ctx', 'tp'))
- input_grads: float32 [2, 6, 2, 1024, 1024], P('section', None, None, ('ctx', 'tp'))
- adapter_in_grad: float32 [2, 1024, 512], P('section', None, 'tp')
- adapter_in_bias_grad: float32 [2, 512], P('section', 'tp')
- adapter_out_grad: float32 [2, 512, 1024], P('section', 'tp')
- adapter_out_bias_grad: float32 [2, 1024], P('section')
Inputs may be any that keep to these rules, and one draw needn't show every extreme that they name: Along each row the ids never fall. In every micro-batch one row, drawn, holds the single id 0 in both src_seg and tgt_seg; every other row holds each of the ids 0 to 3 in both arrays. Every id of a row of tgt_seg also appears in the same row of src_seg, and the reverse. `cross_weights`: independent entries of mean zero.
All inputs are finite; a program needn't handle non-finite values.
Results may differ from a plain program's by a relative error of at most 0.022.
Values may be sent and summed in bfloat16 or wider, within the bound.
A program may use at most 576 MiB of HBM per device.

v0:
```python
import functools

import jax
import jax.numpy as jnp
from jax import lax
from jax.experimental import pallas as pl
from jax.experimental.pallas import tpu as pltpu
from jax.sharding import PartitionSpec as P

HEAD = 64
SCALE = HEAD**-0.5
EPS = 1e-05
MASKED = -1e30
F32 = jnp.float32
BF16 = jnp.bfloat16
SECTION, CTX, TP = "section", "ctx", "tp"


def swap(value):
    return lax.ppermute(value, SECTION, [(0, 1), (1, 0)])


def remote(src, dst, send, recv, where):
    return pltpu.make_async_remote_copy(
        src_ref=src,
        dst_ref=dst,
        send_sem=send,
        recv_sem=recv,
        device_id=where,
        device_id_type=pl.DeviceIdType.MESH,
    )


def device_of(section, chip):
    return (section, chip // 4, lax.rem(chip, 4))


def greet_all():
    s = lax.axis_index(SECTION)
    chip = lax.axis_index(CTX) * 4 + lax.axis_index(TP)
    barrier = pltpu.get_barrier_semaphore()
    for core in (0, 1):
        for i in range(core, 16):
            pl.semaphore_signal(
                barrier,
                1,
                device_id=device_of(lax.rem(s + 1 - core, 2), lax.rem(chip + i, 16)),
                device_id_type=pl.DeviceIdType.MESH,
            )
    pl.semaphore_wait(barrier, 31)


class Scatter:
    BRING = 2

    def __init__(self, arrays, rows, call_id):
        self.inputs = [a for a, _ in arrays]
        self.kinds = [k for _, k in arrays]
        self.rows = rows
        self.call_id = call_id
        self.shapes = [
            jax.ShapeDtypeStruct(
                ((16,) if k == self.BRING else (rows, 2)) + a.shape[1:], a.dtype
            )
            for a, k in arrays
        ]
        count = len(arrays)
        self.scratch = [
            pltpu.SemaphoreType.DMA((count, 16)),
            pltpu.SemaphoreType.DMA((count, 16, 2)),
        ]

    def sends(self, ins, outs, sems):
        send, recv = sems
        s = lax.axis_index(SECTION)
        chip = lax.axis_index(CTX) * 4 + lax.axis_index(TP)
        for a, kind in enumerate(self.kinds):
            for i in range(16):
                p = lax.rem(chip + i, 16)
                if kind == self.BRING:
                    ready = p < self.rows
                    src = ins[a].at[jnp.minimum(p, self.rows - 1)]
                    dst = outs[a].at[chip]
                    core, mark = s, 0
                    stays = True
                else:
                    ready = chip < self.rows
                    src = ins[a].at[p]
                    dst = outs[a].at[jnp.minimum(chip, self.rows - 1), s]
                    core, mark = kind, s
                    stays = s == kind
                near = pltpu.make_async_copy(src, dst, send.at[a, i])
                far = remote(
                    src, dst, send.at[a, i], recv.at[a, i, mark], device_of(core, p)
                )
                yield i, ready, stays, near, far

    def start(self, ins, outs, sems):
        greet_all()
        for i, ready, stays, near, far in self.sends(ins, outs, sems):

            @pl.when(ready)
            def _():
                if i:
                    far.start()
                elif stays is True:
                    near.start()
                else:
                    pl.when(stays)(near.start)
                    pl.when(jnp.logical_not(stays))(far.start)

    def finish(self, ins, outs, sems):
        send, recv = sems
        s = lax.axis_index(SECTION)
        chip = lax.axis_index(CTX) * 4 + lax.axis_index(TP)
        for i, ready, stays, near, far in self.sends(ins, outs, sems):

            @pl.when(ready)
            def _():
                if i:
                    far.wait_send()
                elif stays is True:
                    near.wait()
                else:
                    pl.when(stays)(near.wait)
                    pl.when(jnp.logical_not(stays))(far.wait_send)

        def got(region, sem):
            remote(region, region, send.at[0, 0], sem, (1 - s, 0, 0)).wait_recv()

        for a, kind in enumerate(self.kinds):
            for i in range(16):
                sender = lax.rem(chip + 16 - i, 16)
                if kind == self.BRING:
                    if i:

                        @pl.when(chip < self.rows)
                        def _():
                            got(outs[a].at[sender], recv.at[a, i, 0])

                    continue

                @pl.when((s == kind) & (sender < self.rows))
                def _():
                    for core in (0, 1) if i else (1 - kind,):
                        region = outs[a].at[jnp.minimum(sender, self.rows - 1), core]
                        got(region, recv.at[a, i, core])


def send_kernel(rider, *refs):
    n = len(rider.inputs)
    block_in, (own, spread_out) = refs[n], (refs[n], refs[2 * n + 1])
    ins, outs = refs[:n], refs[n + 1 : 2 * n + 1]
    sems = refs[2 * n + 2 : 2 * n + 4]
    b_send, b_recv = refs[2 * n + 4 :]
    rider.start(ins, outs, sems)
    s = lax.axis_index(SECTION)
    c = lax.axis_index(CTX)
    t = lax.axis_index(TP)
    dst = spread_out.at[c]
    keep = pltpu.make_async_copy(own, dst, b_send.at[0])
    keep.start()
    ways = [
        remote(own, dst, b_send.at[j], b_recv.at[j], (s, lax.rem(c + j, 4), t))
        for j in (1, 2, 3)
    ]
    for way in ways:
        way.start()
    keep.wait()
    for j, way in enumerate(ways):
        way.wait_send()
        region = spread_out.at[lax.rem(c + 3 - j, 4)]
        remote(region, region, b_send.at[0], b_recv.at[j + 1], (s, c, t)).wait_recv()
    rider.finish(ins, outs, sems)


def send_call(rider, block):
    anywhere = pl.BlockSpec(memory_space=pl.ANY)
    count = len(rider.inputs)
    result = pl.pallas_call(
        functools.partial(send_kernel, rider),
        in_specs=[anywhere] * (count + 1),
        out_specs=[anywhere] * (count + 1),
        out_shape=rider.shapes + [jax.ShapeDtypeStruct((4,) + block.shape, block.dtype)],
        scratch_shapes=rider.scratch
        + [pltpu.SemaphoreType.DMA((4,)), pltpu.SemaphoreType.DMA((4,))],
        compiler_params=pltpu.CompilerParams(
            collective_id=rider.call_id, has_side_effects=True
        ),
        name="send_last",
    )(*rider.inputs, block)
    return result[:count], result[count]


def dot_nt(left, right, **kw):
    return lax.dot_general(
        left, right, (((1,), (1,)), ((), ())), preferred_element_type=F32, **kw
    )


def dot_nn(left, right):
    return lax.dot_general(
        left, right, (((1,), (0,)), ((), ())), preferred_element_type=F32
    )


def dot_tn(left, right):
    return lax.dot_general(
        left, right, (((0,), (0,)), ((), ())), preferred_element_type=F32
    )


def attn_fwd_kernel(
    causal, q_ref, ko_ref, kx_ref, vo_ref, vx_ref, fq, fo, fx, qi_ref, ki_ref, o_ref, lse_ref
):
    for pair in range(lse_ref.shape[1]):
        attend_pair(
            0,
            pair,
            q_ref,
            (ko_ref, kx_ref),
            (vo_ref, vx_ref),
            o_ref,
            lse_ref,
            (fq, fo, fx),
            (qi_ref[:, 1:2], (ki_ref[1:2, :], ki_ref[3:4, :])),
            causal,
        )


def attention_call(kernel, name, causal, blocks, small, outs):
    def group_spec(v):
        return pl.BlockSpec((1,) + v.shape[1:], lambda t: (t,) + (0,) * (len(v.shape) - 1))

    return pl.pallas_call(
        functools.partial(kernel, causal),
        grid=(blocks[0].shape[0],),
        in_specs=[group_spec(v) for v in blocks]
        + [pl.BlockSpec(v.shape, lambda t: (0, 0)) for v in small],
        out_specs=[group_spec(v) for v in outs],
        out_shape=outs,
        compiler_params=pltpu.CompilerParams(vmem_limit_bytes=48 * 2**20),
        name=name,
    )(*blocks, *small)


def id_columns(ids, keys):
    lane = jnp.arange(2 * HEAD, dtype=jnp.int32)[None] % HEAD
    same = ids[:, None] == lane
    value = jnp.where(same, 1.0, 0.0) if keys else jnp.where(same, 0.0, MASKED)
    return jnp.where(lane < 4, value, 0.0).astype(BF16)


def attention_forward(q, keys, ids, causal):
    groups, length, width = q.shape
    pairs = width // HEAD // 2
    outs = [
        jax.ShapeDtypeStruct(q.shape, BF16),
        jax.ShapeDtypeStruct((groups, pairs, 2, length), F32),
    ]
    feats = [
        id_columns(ids[0][:, 0], False),
        id_columns(ids[1][0], True),
        id_columns(ids[1][2], True),
    ]
    o, lse = attention_call(
        attn_fwd_kernel, "attn_fwd", causal, [q, *keys], [*feats, *ids], outs
    )
    return o, lse.reshape(groups, 2 * pairs, length)


def attend_back_group(ins, dq_out, dk_outs, dv_outs, qi_ref, ki_ref, causal):
    q_ref, k_refs, v_refs, o_ref, do_ref, lse_ref = ins
    length = q_ref.shape[1]
    heads = q_ref.shape[2] // HEAD
    block = length // 2
    segq = qi_ref[0:1, :]
    posq = qi_ref[1:2, :]
    ones = jnp.ones((8, HEAD), F32)

    def put(out, rows, cols, value):
        out[0][out[1], rows, cols] = value.astype(out[0].dtype)

    for h in range(heads):
        cols = slice(h * HEAD, (h + 1) * HEAD)
        q_all = q_ref[0, :, cols] * jnp.asarray(SCALE, BF16)
        do_all = do_ref[0, :, cols]
        prod = do_all.astype(F32) * o_ref[0, :, cols].astype(F32)
        delta = dot_nt(ones, prod, precision=lax.Precision.HIGHEST)[0:1]
        lse = lse_ref[0, h : h + 1, :]
        dq = [jnp.zeros((block, HEAD), F32), jnp.zeros((block, HEAD), F32)]
        for n in range(2):
            i = 2 * n
            for b in range(2):
                rows = slice(b * block, (b + 1) * block)
                first = b * block if causal else 0
                q = q_all[first:]
                do = do_all[first:]
                k = k_refs[n][0, rows, cols]
                s = dot_nt(k, q)
                ok = ki_ref[rows, i : i + 1] == segq[:, first:]
                if causal:
                    ok = ok & (posq[:, first:] >= ki_ref[rows, i + 1 : i + 2])
                p = jnp.where(ok, jnp.exp(s - lse[:, first:]), 0.0)
                dp = dot_nt(v_refs[n][0, rows, cols], do)
                ds = (p * (dp - delta[:, first:])).astype(BF16)
                put(dv_outs[n], rows, cols, dot_nn(p.astype(BF16), do))
                put(dk_outs[n], rows, cols, dot_nn(ds, q))
                part = dot_tn(ds, k)
                if first:
                    dq[1] = dq[1] + part
                else:
                    dq[0] = dq[0] + part[:block]
                    dq[1] = dq[1] + part[block:]
        put(dq_out, slice(0, block), cols, dq[0] * SCALE)
        put(dq_out, slice(block, length), cols, dq[1] * SCALE)


def attn_bwd_kernel(
    causal,
    q_ref,
    ko_ref,
    kx_ref,
    vo_ref,
    vx_ref,
    o_ref,
    do_ref,
    lse_ref,
    qi_ref,
    ki_ref,
    dq_ref,
    dko_ref,
    dkx_ref,
    dvo_ref,
    dvx_ref,
):
    attend_back_group(
        (q_ref, (ko_ref, kx_ref), (vo_ref, vx_ref), o_ref, do_ref, lse_ref),
        (dq_ref, 0),
        ((dko_ref, 0), (dkx_ref, 0)),
        ((dvo_ref, 0), (dvx_ref, 0)),
        qi_ref,
        ki_ref,
        causal,
    )


def attention_backward(q, keys, o, do, lse, ids, causal):
    outs = [jax.ShapeDtypeStruct(q.shape, BF16)] * 5
    return attention_call(
        attn_bwd_kernel, "attn_bwd", causal, [q, *keys, o, do, lse], ids, outs
    )


def norm(value):
    mean = jnp.mean(value, axis=-1, keepdims=True)
    centered = value - mean
    rstd = lax.rsqrt(jnp.mean(centered * centered, axis=-1, keepdims=True) + EPS)
    return centered * rstd, rstd


def norm_back(normed, rstd, grad):
    return rstd * (
        grad
        - jnp.mean(grad, axis=-1, keepdims=True)
        - normed * jnp.mean(grad * normed, axis=-1, keepdims=True)
    )


def project(rows, weight):
    return jnp.einsum("pk,tkm->tpm", rows, weight, preferred_element_type=F32)


def unproject(blocks, weight):
    return jnp.einsum("tpm,tkm->pk", blocks, weight, preferred_element_type=F32)


def self_forward(rows_bf, rows, w_attn, ids, causal):
    kv = [project(rows_bf, w_attn[:, j]).astype(BF16) for j in (1, 2)]
    other = swap(jnp.stack(kv))
    q = project(rows_bf, w_attn[:, 0]).astype(BF16)
    keys = (kv[0], other[0], kv[1], other[1])
    o, lse = attention_forward(q, keys, ids[0], causal)
    h, rstd = norm(rows + unproject(o, w_attn[:, 3]))
    return h, (q, keys, o, lse, h, rstd)


def attend_back(q, keys, o, do, lse, ids, causal):
    dq, dko, dkx, dvo, dvx = attention_backward(q, keys, o, do, lse, ids[1], causal)
    other = swap(jnp.stack([dkx, dvx])).astype(F32)
    dk = (dko.astype(F32) + other[0]).astype(BF16)
    dv = (dvo.astype(F32) + other[1]).astype(BF16)
    return dq, dk, dv


def self_backward(grad, kept, w_attn, ids, causal):
    q, keys, o, lse, h, rstd = kept
    dpre = norm_back(h, rstd, grad)
    do = project(dpre.astype(BF16), w_attn[:, 3]).astype(BF16)
    dq, dk, dv = attend_back(q, keys, o, do, lse, ids, causal)
    return (
        unproject(dq, w_attn[:, 0])
        + unproject(dk, w_attn[:, 1])
        + unproject(dv, w_attn[:, 2])
        + dpre
    )


def tail_forward(h, tail_w):
    w_in, w_out, a_in, b_in, a_out, b_out = tail_w
    rows = h.astype(BF16)
    inner = project(rows, w_in)
    phi = 0.5 * (1.0 + lax.erf(inner * 0.7071067811865476))
    g = (inner * phi).astype(BF16)
    slope = phi + inner * jnp.exp(inner * inner * -0.5) * 0.3989422804014327
    pre = project(rows, a_in) + b_in.astype(F32)[:, None, :]
    sig = jax.nn.sigmoid(pre)
    s = (pre * sig).astype(BF16)
    a_slope = sig * (1.0 + pre * (1.0 - sig))
    total = jnp.einsum("tpm,tmk->pk", g, w_out, preferred_element_type=F32)
    total += 4.0 * (
        jnp.einsum("tpm,tkm->pk", s, a_out, preferred_element_type=F32)
        + b_out.astype(F32)
    )
    y, rstd = norm(h + total)
    return y, (rows, slope.astype(BF16), s, a_slope.astype(BF16), y, rstd)


def tail_backward(grad, kept, tail_w):
    w_in, w_out, a_in, b_in, a_out, b_out = tail_w
    rows, slope, s, a_slope, y, rstd = kept
    dpre = norm_back(y, rstd, grad)
    db = dpre.astype(BF16)
    dg = jnp.einsum("pk,tmk->tpm", db, w_out, preferred_element_type=F32)
    df = (dg * slope.astype(F32)).astype(BF16)
    ds = 4.0 * jnp.einsum("pk,tkm->tpm", db, a_out, preferred_element_type=F32)
    du = (ds * a_slope.astype(F32)).astype(BF16)
    terms = (
        jnp.einsum("pk,tpm->tkm", rows, du, preferred_element_type=F32),
        jnp.sum(du.astype(F32), axis=1),
        4.0 * jnp.einsum("pk,tpm->tkm", db, s, preferred_element_type=F32),
        4.0 * jnp.sum(db.astype(F32), axis=0),
    )
    return unproject(df, w_in) + unproject(du, a_in) + dpre, terms


def head_mask(rows, j):
    lane = lax.broadcasted_iota(jnp.int32, (rows, 2 * HEAD), 1)
    return (lane < HEAD) if j == 0 else (lane >= HEAD)


def attend_pair(t, pair, q_ref, k_refs, v_refs, o_ref, lse_ref, feats, places, causal):
    length = q_ref.shape[1]
    block = length // 2
    lanes = pl.ds(pl.multiple_of(pair * 2 * HEAD, 2 * HEAD), 2 * HEAD)
    posq, posk = places
    for b in range(2):
        rows = slice(b * block, (b + 1) * block)
        q2 = q_ref[t, rows, lanes] * jnp.asarray(SCALE, BF16)
        cuts = [(n, a) for n in range(2) for a in range(b + 1 if causal else 2)]
        outs = []
        for j in range(2):
            q = jnp.where(head_mask(block, j), q2, feats[0][rows])
            parts = []
            for n, a in cuts:
                span = slice(a * block, (a + 1) * block)
                k = jnp.where(
                    head_mask(block, j), k_refs[n][t, span, lanes], feats[1 + n][span]
                )
                s = dot_nt(q, k)
                if causal and a == b:
                    s = jnp.where(posq[rows] >= posk[n][:, span], s, MASKED)
                parts.append(s)
            top = functools.reduce(
                jnp.maximum, [jnp.max(s, axis=1, keepdims=True) for s in parts]
            )
            ex = [jnp.exp(s - top) for s in parts]
            total = sum(jnp.sum(e, axis=1, keepdims=True) for e in ex)
            out = sum(
                dot_nn(
                    e.astype(BF16), v_refs[n][t, a * block : (a + 1) * block, lanes]
                )
                for e, (n, a) in zip(ex, cuts)
            )
            outs.append(out / total)
            lse = top + jnp.log(total)
            lse_ref[t, pair, j : j + 1, rows] = jnp.broadcast_to(lse, (block, 128)).T[
                0:1
            ]
        o_ref[t, rows, lanes] = jnp.where(head_mask(block, 0), *outs).astype(BF16)


ATTN, FFN_IN, FFN_OUT, ADAPTER, CROSS = range(5)
ORDER = (
    (0, ATTN),
    (1, ATTN),
    (0, FFN_IN),
    (0, FFN_OUT),
    (0, ADAPTER),
    (0, CROSS),
    (1, CROSS),
    (1, FFN_IN),
    (1, FFN_OUT),
    (1, ADAPTER),
)
(
    ENC_QKV,
    ENC_ATTN,
    ENC_OUT,
    DEC_QKV,
    DEC_ATTN,
    DEC_OUT,
    HIDDEN,
    GATED,
    MEMORY,
    CROSS_Q,
    CROSS_ATTN,
    CROSS_OUT,
    END,
) = range(13)
WORK = (
    (ENC_QKV, 4, (0, ATTN), 2.0),
    (ENC_ATTN, 8, None, 2.3),
    (ENC_OUT, 1, None, 4.0),
    (DEC_QKV, 4, (1, ATTN), 2.0),
    (DEC_ATTN, 8, None, 2.1),
    (DEC_OUT, 1, None, 4.0),
    (HIDDEN, 8, (0, FFN_OUT), 2.5),
    (GATED, 1, (0, ADAPTER), 4.0),
    (MEMORY, 4, (0, CROSS), 1.5),
    (CROSS_Q, 1, (1, CROSS), 4.0),
    (CROSS_ATTN, 8, None, 2.3),
    (CROSS_OUT, 1, None, 4.0),
    (END, 1, (1, ADAPTER), 0.0),
)


def plan_steps(sizes):
    ready, clock = [], 20.0
    for e, g in ORDER:
        for _ in range(3):
            clock += sizes[g] / 3 * 14e-6
            ready.append(clock)
    ticks = len(ready) + 2
    ready += [clock + 4, clock + 8]
    starts, at, step, now, done = {}, {}, 0, 0.0, 0
    for name, count, need, cost in WORK:
        starts[name] = step
        for n in range(count):
            while done < ticks and (
                ready[done] <= now
                or (need and done <= 3 * ORDER.index(need) + 4)
            ):
                at[done] = step
                now = max(now, ready[done])
                done += 1
            now += cost
            step += 1
    for n in range(done, ticks):
        at[n] = step - 1
    return starts, at, step


HEADS, LSE, WIDE, RSTD, LANES = range(5)
(
    EQ,
    EK,
    EKX,
    EV,
    EVX,
    EO,
    EL,
    EH,
    ER,
    ES,
    EA,
    EY,
    EYR,
    DQ,
    DK,
    DKX,
    DV,
    DVX,
    DO,
    DL,
    DH,
    DR,
    MK,
    MKX,
    MV,
    MVX,
    CQ,
    CO,
    CL,
    C2,
    C2R,
) = range(31)
KEPT = {
    EQ: HEADS,
    EK: HEADS,
    EKX: HEADS,
    EV: HEADS,
    EVX: HEADS,
    EO: HEADS,
    EL: LSE,
    EH: WIDE,
    ER: RSTD,
    ES: LANES,
    EA: LANES,
    EY: WIDE,
    EYR: RSTD,
    DQ: HEADS,
    DK: HEADS,
    DKX: HEADS,
    DV: HEADS,
    DVX: HEADS,
    DO: HEADS,
    DL: LSE,
    DH: WIDE,
    DR: RSTD,
    MK: HEADS,
    MKX: HEADS,
    MV: HEADS,
    MVX: HEADS,
    CQ: HEADS,
    CO: HEADS,
    CL: LSE,
    C2: WIDE,
    C2R: RSTD,
}


def forward_kernel(plan, rows, *refs):
    starts, tick_step, steps = plan
    refs = list(refs)

    def take(count):
        got = refs[:count]
        del refs[:count]
        return got

    shards = take(5)
    tokens = take(2)
    col_ref, row_ref, feat_ref = take(3)
    full = (take(5), take(5))
    (slope_out,) = take(1)
    kept_out = take(len(KEPT))
    kept = take(len(KEPT))
    xs = take(2)
    wb, wi, wo, wad, slope = take(5)
    store_a, store_f = take(2)
    (
        z_send,
        z_recv,
        n_send,
        n_recv,
        f_send,
        f_recv,
        s_send,
        s_recv,
        own_sem,
        t_send,
        t_recv,
        kv_send,
        kv_recv,
        load_sem,
        out_sem,
        slope_sem,
    ) = refs
    step = pl.program_id(0)
    s = lax.axis_index(SECTION)
    c = lax.axis_index(CTX)
    t = lax.axis_index(TP)
    chips = 16
    chip = c * 4 + t
    cx = c + 1 - 2 * lax.rem(c, 2)
    cy = lax.rem(c + 2, 4)
    cd = 3 - c
    sib = (1 - s, c, t)

    def xor(k):
        return {1: t + 1 - 2 * lax.rem(t, 2), 2: lax.rem(t + 2, 4), 3: 3 - t}[k]

    def token_copy(kind, i):
        p = lax.rem(chip + i, chips)
        src = tokens[kind].at[jnp.minimum(p, rows - 1)]
        dst = xs[kind].at[chip]
        if i == 0:
            return p, pltpu.make_async_copy(src, dst, t_send.at[kind, 0])
        return p, remote(
            src, dst, t_send.at[kind, i], t_recv.at[kind, i], device_of(s, p)
        )

    def send_tokens(kind):
        for i in range(chips):
            p, copy = token_copy(kind, i)
            pl.when(p < rows)(copy.start)

    def got(region, sem):
        remote(region, region, load_sem.at[0], sem, sib).wait_recv()

    def wait_tokens(kind):
        for i in range(chips):
            p, copy = token_copy(kind, i)
            pl.when(p < rows)(copy.wait if i == 0 else copy.wait_send)
            if i:

                @pl.when(chip < rows)
                def _():
                    got(
                        xs[kind].at[lax.rem(chip + chips - i, chips)],
                        t_recv.at[kind, i],
                    )

    items = [(n, k) for n in range(len(ORDER)) for k in (1, 2, 3)]
    window = 4

    def block(n, who, h, q, u=None):
        e, g = ORDER[n]
        size = shards[g].shape[0]
        start = h * (size // 2) + q * (size // 8)
        length = size // 8
        if u is not None:
            length = size // 16
            start = start + u * length
        return full[e][g].at[who, pl.ds(pl.multiple_of(start, 16), length)]

    def z_copy(n, k, h):
        g = ORDER[n][1]
        size = shards[g].shape[0]
        start = h * (size // 2) + c * (size // 8)
        return remote(
            shards[g].at[pl.ds(pl.multiple_of(start, 16), size // 8)],
            block(n, t, h, c),
            z_send.at[n, k - 1, h],
            z_recv.at[n, k - 1],
            (h, c, xor(k)),
        )

    def store(g):
        if g in (FFN_IN, FFN_OUT):
            return store_f
        return store_a.at[pl.ds(0, shards[g].shape[0])]

    def fetch(n):
        g = ORDER[n][1]
        return pltpu.make_async_copy(shards[g], store(g), own_sem.at[n, 3])

    def put(n):
        e, g = ORDER[n]
        return pltpu.make_async_copy(store(g), full[e][g].at[t], own_sem.at[n, 0])

    def far(n):
        e, g = ORDER[n]
        return remote(
            shards[g], full[e][g].at[t], own_sem.at[n, 1], own_sem.at[n, 2], sib
        )

    def before(n):
        e, g = ORDER[n]
        pool = (FFN_IN, FFN_OUT) if g in (FFN_IN, FFN_OUT) else (ATTN, ADAPTER, CROSS)
        olds = [m for m in range(n) if ORDER[m][0] == e and ORDER[m][1] in pool]
        return olds[-1] if olds else None

    def start_z(i):
        n, k = items[i]

        @pl.when(s == ORDER[n][0])
        def _():
            if k == 1:
                far(n).start()
            for h in range(2):
                z_copy(n, k, h).start()

    def near_copy(n, k, j):
        src = block(n, xor(k), s, c)
        return remote(
            src,
            src,
            n_send.at[n, k - 1, j],
            n_recv.at[n, k - 1, j],
            (s, (cx, cy)[j], t),
        )

    def sibling_copy(n, k, j):
        src = block(n, xor(k), s, (c, cx, cy, cd)[j])
        return remote(src, src, s_send.at[n, k - 1, j], s_recv.at[n, k - 1, j], sib)

    def forward_copy(n, k, j):
        src = block(n, xor(k), s, (cx, cy)[j], j)
        return remote(
            src,
            src,
            f_send.at[n, k - 1, j],
            f_recv.at[n, k - 1, j],
            (s, (cy, cx)[j], t),
        )

    def stage2(i):
        n, k = items[i]
        got(block(n, xor(k), s, c), z_recv.at[n, k - 1])
        near_copy(n, k, 0).start()
        near_copy(n, k, 1).start()
        sibling_copy(n, k, 0).start()
        if k == 2:
            return

        @pl.when(s == ORDER[n][0])
        def _():
            if k == 1:
                old = before(n)
                if old is not None and not put_read_first(old, i):
                    put(old).wait()
                fetch(n).start()
            else:
                fetch(n).wait()
                put(n).start()

    def stage3(i):
        n, k = items[i]
        for j, q in ((0, cx), (1, cy)):
            got(block(n, xor(k), s, q), n_recv.at[n, k - 1, j])
            forward_copy(n, k, j).start()
            sibling_copy(n, k, j + 1).start()

    def stage4(i):
        n, k = items[i]
        for u in range(2):
            got(block(n, xor(k), s, cd, u), f_recv.at[n, k - 1, u])
        sibling_copy(n, k, 3).start()

    count = len(items)

    def tick(i):
        if i < count:
            stage2(i)
            if i + window < count:
                start_z(i + window)
        if 0 <= i - 1 < count:
            stage3(i - 1)
        if 0 <= i - 2 < count:
            stage4(i - 2)
        if i == 3:
            send_tokens(1)

    def arrive_step(n):
        for name, _, need, _ in WORK[:-1]:
            if need == ORDER[n]:
                return starts[name]
        return starts[HIDDEN] if ORDER[n] == (0, FFN_IN) else steps - 1

    def put_read_first(n, i):
        return arrive_step(n) < tick_step[i]

    def put_left(n):
        after = [m for m in range(len(ORDER)) if before(m) == n]
        return not after or put_read_first(n, 3 * after[0])

    def arrive(n):
        e, g = ORDER[n]
        for k in (1, 2, 3):
            for j, q in enumerate((c, cx, cy, cd)):
                got(block(n, xor(k), 1 - s, q), s_recv.at[n, k - 1, j])

        @pl.when(s == e)
        def _():
            if put_left(n):
                put(n).wait()

        @pl.when(s != e)
        def _():
            got(full[e][g].at[t], own_sem.at[n, 2])

    @pl.when(step == 0)
    def _():
        greet_all()
        send_tokens(0)
        for i in range(window):
            start_z(i)

    for i in range(count + 2):
        pl.when(step == tick_step[i])(functools.partial(tick, i))

    def on(name):
        first = starts[name]
        last = first + [w[1] for w in WORK if w[0] == name][0]
        need = [w[2] for w in WORK if w[0] == name][0]
        if need and name != END:
            pl.when(step == first)(functools.partial(arrive, ORDER.index(need)))
        return step - first, pl.when((step >= first) & (step < last))

    def load(src, dst, slot=0):
        return pltpu.make_async_copy(src, dst, load_sem.at[slot])

    def keep(*names):
        for n in names:
            pltpu.make_async_copy(kept[n], kept_out[n], out_sem.at[n]).start()

    attn_rows = full[0][ATTN].shape[1] // 4

    def kv_copies(which, g, names):
        k, kx, v, vx = names
        return [
            remote(
                kept[a].at[g], kept[b].at[g], kv_send.at[which, g, j], kv_recv.at[which, g, j], sib
            )
            for j, (a, b) in enumerate(((k, kx), (v, vx)))
        ]

    def projections(name, which, e, g_id, x, names):
        i, when = on(name)
        tiles = len(names)
        height = tiles * attn_rows

        def source(j):
            return full[e][g_id].at[j, pl.ds(0, height)]

        @when
        def _():
            slot = lax.rem(i, 2)

            @pl.when(i == 0)
            def _():
                load(source(0), wb.at[0, pl.ds(0, height)]).start()

            load(source(0), wb.at[slot, pl.ds(0, height)]).wait()

            @pl.when(i < 3)
            def _():
                load(source(jnp.minimum(i + 1, 3)), wb.at[1 - slot, pl.ds(0, height)]).start()

            rows_in = x()
            for n, name_out in enumerate(names):
                w = wb[slot, n * attn_rows : (n + 1) * attn_rows, :]
                kept[name_out][i] = dot_nn(rows_in, w).astype(BF16)
            for copy in kv_copies(which, i, keys_of[which]):
                copy.start()

    keys_of = (
        (EK, EKX, EV, EVX),
        (DK, DKX, DV, DVX),
        (MK, MKX, MV, MVX),
    )

    def attend(name, which, q, o, lse, feats, causal):
        i, when = on(name)
        k, kx, v, vx = keys_of[which]

        @when
        def _():
            g, pair = i // 2, lax.rem(i, 2)

            @pl.when(pair == 0)
            def _():
                for copy in kv_copies(which, g, keys_of[which]):
                    copy.wait_send()
                    copy.wait_recv()

            attend_pair(
                g,
                pair,
                kept[q],
                (kept[k], kept[kx]),
                (kept[v], kept[vx]),
                kept[o],
                kept[lse],
                [feat_ref.at[f] for f in feats],
                (col_ref[...], (row_ref[0:1, :], row_ref[1:2, :])),
                causal,
            )

            @pl.when(i == 7)
            def _():
                keep(q, k, kx, v, vx, o, lse)

    def tiles4(e, g_id, first_row):
        copies = [
            load(
                full[e][g_id].at[j, pl.ds(first_row, attn_rows)],
                wb.at[0, pl.ds(j * attn_rows, attn_rows)],
                j,
            )
            for j in range(4)
        ]
        for copy in copies:
            copy.start()
        for copy in copies:
            copy.wait()

    def out_norm(name, e, g_id, first_row, residual, source, wide, rstd_name):
        _, when = on(name)

        @when
        def _():
            tiles4(e, g_id, first_row)
            total = residual()
            for j in range(4):
                total = total + dot_nt(
                    kept[source][j], wb[0, j * attn_rows : (j + 1) * attn_rows, :]
                )
            normed, rstd = norm(total)
            kept[wide][...] = normed
            kept[rstd_name][...] = jnp.broadcast_to(rstd, kept[rstd_name].shape)
            keep(wide, rstd_name)

    def flat_x(n):
        shape = xs[n].shape
        return xs[n][...].reshape(shape[0] * shape[1], shape[2])

    blocks = (
        (ENC_QKV, ENC_ATTN, ENC_OUT, EQ, EK, EV, EO, EL, EH, ER, (0, 1, 2)),
        (DEC_QKV, DEC_ATTN, DEC_OUT, DQ, DK, DV, DO, DL, DH, DR, (3, 4, 5)),
    )
    for e, (qkv, attn, out, q, k, v, o, lse, h, r, feats) in enumerate(blocks):
        pl.when(step == starts[qkv])(functools.partial(wait_tokens, e))
        projections(qkv, e, e, ATTN, functools.partial(flat_x, e), (q, k, v))
        attend(attn, e, q, o, lse, feats, e == 1)
        residual = lambda e=e: flat_x(e).astype(F32)
        out_norm(out, e, ATTN, 3 * attn_rows, residual, o, h, r)

    i, when = on(HIDDEN)
    hidden = wi.shape[2]

    @pl.when(step == starts[HIDDEN])
    def _():
        arrive(ORDER.index((0, FFN_IN)))

    def ffn_loads(j, slot):
        g, u = j // 2, lax.rem(j, 2)
        span = pl.ds(pl.multiple_of(u * hidden, 128), hidden)
        return (
            load(full[0][FFN_IN].at[g, :, span], wi.at[slot], 2 * slot),
            load(full[0][FFN_OUT].at[g, span], wo.at[slot], 2 * slot + 1),
        )

    def slope_copy(j, slot):
        g, u = j // 2, lax.rem(j, 2)
        span = pl.ds(pl.multiple_of(u * hidden, 128), hidden)
        return pltpu.make_async_copy(
            slope.at[slot], slope_out.at[g, :, span], slope_sem.at[slot]
        )

    @when
    def _():
        slot = lax.rem(i, 2)

        @pl.when(i == 0)
        def _():
            for copy in ffn_loads(0, 0):
                copy.start()
            kept[EY][...] = jnp.zeros_like(kept[EY])

        for copy in ffn_loads(i, slot):
            copy.wait()

        @pl.when(i < 7)
        def _():
            for copy in ffn_loads(i + 1, 1 - slot):
                copy.start()

        @pl.when(i >= 2)
        def _():
            slope_copy(i - 2, slot).wait()

        inner = dot_nn(kept[EH][...].astype(BF16), wi[slot])
        phi = 0.5 * (1.0 + lax.erf(inner * 0.7071067811865476))
        slope[slot] = (
            phi + inner * jnp.exp(inner * inner * -0.5) * 0.3989422804014327
        ).astype(BF16)
        slope_copy(i, slot).start()
        kept[EY][...] += dot_nn((inner * phi).astype(BF16), wo[slot])

    i, when = on(GATED)

    @when
    def _():
        for j in range(2):
            slope_copy(6 + j, j).wait()
        copy = load(full[0][ADAPTER], wad)
        copy.start()
        copy.wait()
        h = kept[EH][...]
        rows_in = h.astype(BF16)
        lanes = wad.shape[2] // 2
        extra = wad[0, attn_rows : attn_rows + 16, :].astype(F32)
        last = jnp.concatenate([extra[1 + r : 2 + r] for r in range(4)], axis=1)
        total = 4.0 * last
        for j in range(4):
            bias = wad[j, attn_rows : attn_rows + 16, :lanes].astype(F32)[0:1]
            pre = dot_nn(rows_in, wad[j, :attn_rows, :lanes]) + bias
            sig = 1.0 / (1.0 + jnp.exp(-pre))
            gated = (pre * sig).astype(BF16)
            kept[ES][j] = gated
            kept[EA][j] = (sig * (1.0 + pre * (1.0 - sig))).astype(BF16)
            total = total + 4.0 * dot_nt(gated, wad[j, :attn_rows, lanes:])
        normed, rstd = norm(h + (kept[EY][...] + total))
        kept[EY][...] = normed
        kept[EYR][...] = jnp.broadcast_to(rstd, kept[EYR].shape)
        keep(ES, EA, EY, EYR)

    projections(MEMORY, 2, 0, CROSS, lambda: kept[EY][...].astype(BF16), (MK, MV))
    _, when = on(CROSS_Q)

    @when
    def _():
        tiles4(1, CROSS, 0)
        rows_in = kept[DH][...].astype(BF16)
        for j in range(4):
            kept[CQ][j] = dot_nn(
                rows_in, wb[0, j * attn_rows : (j + 1) * attn_rows, :]
            ).astype(BF16)

    attend(CROSS_ATTN, 2, CQ, CO, CL, (3, 1, 2), False)
    out_norm(CROSS_OUT, 1, CROSS, attn_rows, lambda: kept[DH][...], CO, C2, C2R)

    @pl.when(step == steps - 1)
    def _():
        for g in (FFN_IN, FFN_OUT, ADAPTER):
            arrive(ORDER.index((1, g)))
        for n, k in items:
            for j in range(2):
                near_copy(n, k, j).wait_send()
                forward_copy(n, k, j).wait_send()
            for j in range(4):
                sibling_copy(n, k, j).wait_send()
        for n in range(len(ORDER)):

            @pl.when(s == ORDER[n][0])
            def _():
                far(n).wait_send()
                for k in (1, 2, 3):
                    for h in range(2):
                        z_copy(n, k, h).wait_send()

        for n in KEPT:
            pltpu.make_async_copy(kept[n], kept_out[n], out_sem.at[n]).wait()


def forward_call(shards, tokens, col, row, feats):
    part, width = tokens[0].shape[1:]
    length = 16 * part
    groups = len(ORDER)
    dma = pltpu.SemaphoreType.DMA
    anywhere = pl.BlockSpec(memory_space=pl.ANY)
    cols = shards[ATTN].shape[1]
    shapes = (
        ((4, length, cols), BF16),
        ((4, cols // HEAD // 2, 2, length), F32),
        ((length, width), F32),
        ((length, 128), F32),
        ((4, length, shards[ADAPTER].shape[1] // 2), BF16),
    )
    kept = [shapes[kind] for kind in KEPT.values()]
    hidden = shards[FFN_IN].shape[1]
    sizes = [
        (groups, 3, 2),
        (groups, 3),
        (groups, 3, 2),
        (groups, 3, 2),
        (groups, 3, 2),
        (groups, 3, 2),
        (groups, 3, 4),
        (groups, 3, 4),
        (groups, 4),
        (2, 16),
        (2, 16),
        (3, 4, 2),
        (3, 4, 2),
        (4,),
        (len(KEPT),),
        (2,),
    ]
    plan = plan_steps([v.size * 2 for v in shards])
    result = pl.pallas_call(
        functools.partial(forward_kernel, plan, tokens[0].shape[0]),
        grid=(plan[2],),
        in_specs=[anywhere] * 7
        + [
            pl.BlockSpec(col.shape, lambda i: (0, 0)),
            pl.BlockSpec(row.shape, lambda i: (0, 0)),
            pl.BlockSpec(feats.shape, lambda i: (0, 0, 0)),
        ],
        out_specs=[anywhere] * (11 + len(KEPT)),
        out_shape=[jax.ShapeDtypeStruct((4,) + v.shape, v.dtype) for v in shards] * 2
        + [jax.ShapeDtypeStruct((4, length, hidden), BF16)]
        + [jax.ShapeDtypeStruct(*v) for v in kept],
        scratch_shapes=[pltpu.VMEM(*v) for v in kept]
        + [pltpu.VMEM((16, part, width), BF16)] * 2
        + [
            pltpu.VMEM((2,) + shards[ATTN].shape, BF16),
            pltpu.VMEM((2, width, hidden // 2), BF16),
            pltpu.VMEM((2, hidden // 2, width), BF16),
            pltpu.VMEM((4,) + shards[ADAPTER].shape, BF16),
            pltpu.VMEM((2, length, hidden // 2), BF16),
            pltpu.VMEM(shards[ATTN].shape, BF16),
            pltpu.VMEM(shards[FFN_IN].shape, BF16),
        ]
        + [dma(size) for size in sizes],
        compiler_params=pltpu.CompilerParams(
            collective_id=0, has_side_effects=True, vmem_limit_bytes=60 * 2**20
        ),
        name="forward",
    )(*shards, *tokens, col, row, feats)
    return result[:5], result[5:10], result[10], result[11:]


def ids_kernel(ids, out, send, recv):
    s = lax.axis_index(SECTION)
    c = lax.axis_index(CTX)
    t = lax.axis_index(TP)
    barrier = pltpu.get_barrier_semaphore()
    for j in (1, 2, 3):
        pl.semaphore_signal(
            barrier,
            1,
            device_id=(s, lax.rem(c + j, 4), t),
            device_id_type=pl.DeviceIdType.MESH,
        )
    pl.semaphore_wait(barrier, 3)
    out[c] = ids[...]
    ways = [
        remote(ids, out.at[c], send.at[j - 1], recv.at[j - 1], (s, lax.rem(c + j, 4), t))
        for j in (1, 2, 3)
    ]
    for way in ways:
        way.start()
    for j, way in enumerate(ways):
        way.wait_send()
        region = out.at[lax.rem(c + 3 - j, 4)]
        remote(region, region, send.at[j], recv.at[j], (s, c, t)).wait_recv()


def ids_call(ids):
    spec = pl.BlockSpec(memory_space=pltpu.VMEM)
    return pl.pallas_call(
        ids_kernel,
        in_specs=[spec],
        out_specs=spec,
        out_shape=jax.ShapeDtypeStruct((4,) + ids.shape, ids.dtype),
        scratch_shapes=[pltpu.SemaphoreType.DMA((3,)), pltpu.SemaphoreType.DMA((3,))],
        compiler_params=pltpu.CompilerParams(collective_id=1, has_side_effects=True),
        name="ids",
    )(ids)


def tail_kernel(rider, *refs):
    refs = list(refs)

    def take(count):
        got = refs[:count]
        del refs[:count]
        return got

    h_ref, w_in_ref, w_out_ref, adapter_ref = take(4)
    ride_ins = take(len(rider.inputs))
    slope_ref, s_ref, a_ref, y_ref, yr_ref, out_ref = take(6)
    ride = (ride_ins, take(len(rider.inputs)), take(len(rider.scratch)))
    rows_in, acc = refs
    step = pl.program_id(0)
    width = acc.shape[1]
    lanes = adapter_ref.shape[2] // 2

    @pl.when(step == 0)
    def _():
        rider.start(*ride)
        extra = adapter_ref[0, width : width + 16, :].astype(F32)
        cuts = width // adapter_ref.shape[2]
        last = jnp.concatenate([extra[1 + r : 2 + r] for r in range(cuts)], axis=1)
        acc[...] = h_ref[...] + 4.0 * last
        rows_in[...] = h_ref[...].astype(BF16)

    @pl.when(step < 4)
    def _():
        bias = adapter_ref[0, width : width + 16, :lanes].astype(F32)[0:1]
        pre = dot_nn(rows_in[...], adapter_ref[0, :width, :lanes]) + bias
        sig = 1.0 / (1.0 + jnp.exp(-pre))
        gated = (pre * sig).astype(BF16)
        s_ref[0] = gated
        a_ref[0] = (sig * (1.0 + pre * (1.0 - sig))).astype(BF16)
        acc[...] += 4.0 * dot_nt(gated, adapter_ref[0, :width, lanes:])

    @pl.when((step >= 4) & (step < 12))
    def _():
        inner = dot_nn(rows_in[...], w_in_ref[0])
        phi = 0.5 * (1.0 + lax.erf(inner * 0.7071067811865476))
        slope_ref[0] = (
            phi + inner * jnp.exp(inner * inner * -0.5) * 0.3989422804014327
        ).astype(BF16)
        acc[...] += dot_nn((inner * phi).astype(BF16), w_out_ref[0])

    @pl.when(step == 12)
    def _():
        normed, rstd = norm(acc[...])
        y_ref[...] = normed
        yr_ref[...] = jnp.broadcast_to(rstd, yr_ref.shape)
        out_ref[...] = normed.astype(BF16)
        rider.finish(*ride)


def tail_call(h, tail_w, rider):
    w_in, w_out, adapter = tail_w
    length, width = h.shape
    groups, _, hidden = w_in.shape
    lanes = adapter.shape[2] // 2
    anywhere = pl.BlockSpec(memory_space=pl.ANY)

    def tile(j):
        j = jnp.clip(j - groups, 0, 7)
        return j // 2, lax.rem(j, 2)

    def group(j):
        return jnp.minimum(j, groups - 1)

    wide = pl.BlockSpec((length, width), lambda j: (0, 0))
    gated = pl.BlockSpec((1, length, lanes), lambda j: (group(j), 0, 0))
    cut = lambda rows: pl.BlockSpec(
        (1, rows, hidden // 2), lambda j: (tile(j)[0], 0, tile(j)[1])
    )
    result = pl.pallas_call(
        functools.partial(tail_kernel, rider),
        grid=(groups + 9,),
        in_specs=[
            wide,
            cut(width),
            pl.BlockSpec((1, hidden // 2, width), lambda j: (tile(j)[0], tile(j)[1], 0)),
            pl.BlockSpec((1,) + adapter.shape[1:], lambda j: (group(j), 0, 0)),
        ]
        + [anywhere] * len(rider.inputs),
        out_specs=[
            cut(length),
            gated,
            gated,
            wide,
            pl.BlockSpec((length, 128), lambda j: (0, 0)),
            wide,
        ]
        + [anywhere] * len(rider.inputs),
        out_shape=[
            jax.ShapeDtypeStruct((groups, length, hidden), BF16),
            jax.ShapeDtypeStruct((groups, length, lanes), BF16),
            jax.ShapeDtypeStruct((groups, length, lanes), BF16),
            jax.ShapeDtypeStruct((length, width), F32),
            jax.ShapeDtypeStruct((length, 128), F32),
            jax.ShapeDtypeStruct((length, width), BF16),
        ]
        + rider.shapes,
        scratch_shapes=rider.scratch
        + [pltpu.VMEM((length, width), BF16), pltpu.VMEM((length, width), F32)],
        compiler_params=pltpu.CompilerParams(
            collective_id=rider.call_id, has_side_effects=True, vmem_limit_bytes=60 * 2**20
        ),
        name="tail",
    )(h, w_in, w_out, adapter, *rider.inputs)
    return result[:6], result[6:]


def norm_back_rows(normed, rstd, grad):
    return rstd * (
        grad
        - jnp.mean(grad, axis=-1, keepdims=True)
        - normed * jnp.mean(grad * normed, axis=-1, keepdims=True)
    )


def head_grads(da, w_ref, do_ref):
    for g in range(w_ref.shape[0]):
        do_ref[g] = dot_nn(da, w_ref[g]).astype(BF16)


def sibling_of():
    return (1 - lax.axis_index(SECTION), lax.axis_index(CTX), lax.axis_index(TP))


def tail_back_kernel(rider, *refs):
    refs = list(refs)

    def take(count):
        got = refs[:count]
        del refs[:count]
        return got

    grad_ref, y_ref, yr_ref, h_ref, hr_ref, slope_ref = take(6)
    w_out_ref, w_in_ref, adapter_ref, s_ref, a_ref, w_do_ref = take(6)
    ride_ins = take(len(rider.inputs))
    dpre_ref, do_ref, pieces_ref, tails_ref = take(4)
    ride = (ride_ins, take(len(rider.inputs)), take(len(rider.scratch)))
    db, acc, mine, away, got, send, recv = refs
    step = pl.program_id(0)
    groups = away.shape[0]
    width = acc.shape[1]
    lanes = adapter_ref.shape[2] // 2
    first = lax.axis_index(SECTION) == 0

    def to_sibling(g):
        return remote(
            away.at[g], got.at[g], send.at[g], recv.at[g], sibling_of()
        )

    @pl.when(step == 0)
    def _():
        rider.start(*ride)
        dpre = norm_back_rows(y_ref[...], yr_ref[:, 0:1], grad_ref[...].astype(F32))
        acc[...] = dpre
        db[...] = dpre.astype(BF16)

    @pl.when(step < groups)
    def _():
        branch = db[...]
        ds = 4.0 * dot_nn(branch, adapter_ref[0, :width, lanes:])
        du = (ds * a_ref[0].astype(F32)).astype(BF16)
        acc[...] += dot_nt(du, adapter_ref[0, :width, :lanes])
        d_in = dot_tn(du, h_ref[...].astype(BF16))
        d_out = 4.0 * dot_tn(s_ref[0], branch)
        last = 4.0 * jnp.sum(branch.astype(F32), axis=0, keepdims=True)
        bias = jnp.sum(du.astype(F32), axis=0, keepdims=True)
        cut = width // 4
        bias = jnp.concatenate([bias, jnp.zeros((1, cut - lanes), F32)], axis=1)
        row = lax.broadcasted_iota(jnp.int32, (16, cut), 0)
        part = lanes // 4
        for c in range(4):
            one = d_in[c * part : (c + 1) * part]
            two = d_out[c * part : (c + 1) * part]
            mine[step, c] = jnp.where(first, one, two)
            away[step, c] = jnp.where(first, two, one).astype(BF16)
            tails_ref[c, step] = jnp.where(
                row == 0,
                last[:, c * cut : (c + 1) * cut],
                jnp.where(row == 1, bias, 0.0),
            ).astype(BF16)
        to_sibling(step).start()

    @pl.when((step >= groups) & (step < groups + 8))
    def _():
        dg = dot_nt(db[...], w_out_ref[0])
        df = (dg * slope_ref[0].astype(F32)).astype(BF16)
        acc[...] += dot_nt(df, w_in_ref[0])

    @pl.when(step == groups + 8)
    def _():
        dpre = norm_back_rows(h_ref[...], hr_ref[:, 0:1], acc[...])
        dpre_ref[...] = dpre
        head_grads(dpre.astype(BF16), w_do_ref, do_ref)
        for g in range(groups):
            copy = to_sibling(g)
            copy.wait_send()
            copy.wait_recv()
            for c in range(4):
                pieces_ref[c, g] = (mine[g, c] + got[g, c].astype(F32)).astype(BF16)
        rider.finish(*ride)


def tail_back(grad, y, yr, h, hr, slope, tail_w, s_act, a_slope, w_do, do_block, rider):
    w_in, w_out, adapter = tail_w
    length, width = y.shape
    groups, _, hidden = slope.shape
    lanes = s_act.shape[2]
    cols = w_do.shape[2]
    part = lanes // 4
    anywhere = pl.BlockSpec(memory_space=pl.ANY)

    def whole(v):
        return pl.BlockSpec(v.shape, lambda j: (0, 0))

    def tile(j):
        j = jnp.clip(j - groups, 0, 7)
        return j // 2, lax.rem(j, 2)

    def group(j):
        return jnp.minimum(j, groups - 1)

    result = pl.pallas_call(
        functools.partial(tail_back_kernel, rider),
        grid=(groups + 9,),
        in_specs=[whole(v) for v in (grad, y, yr, h, hr)]
        + [
            pl.BlockSpec((1, length, hidden // 2), lambda j: (tile(j)[0], 0, tile(j)[1])),
            pl.BlockSpec((1, hidden // 2, width), lambda j: (tile(j)[0], tile(j)[1], 0)),
            pl.BlockSpec((1, width, hidden // 2), lambda j: (tile(j)[0], 0, tile(j)[1])),
            pl.BlockSpec((1,) + adapter.shape[1:], lambda j: (group(j), 0, 0)),
            pl.BlockSpec((1, length, lanes), lambda j: (group(j), 0, 0)),
            pl.BlockSpec((1, length, lanes), lambda j: (group(j), 0, 0)),
            pl.BlockSpec((groups, width, cols), lambda j: (0, do_block, 0)),
        ]
        + [anywhere] * len(rider.inputs),
        out_specs=[
            pl.BlockSpec((length, width), lambda j: (0, 0)),
            pl.BlockSpec((groups, length, cols), lambda j: (0, 0, 0)),
            pl.BlockSpec((4, groups, part, width), lambda j: (0, 0, 0, 0)),
            pl.BlockSpec((4, groups, 16, width // 4), lambda j: (0, 0, 0, 0)),
        ]
        + [anywhere] * len(rider.inputs),
        out_shape=[
            jax.ShapeDtypeStruct((length, width), F32),
            jax.ShapeDtypeStruct((groups, length, cols), BF16),
            jax.ShapeDtypeStruct((4, groups, part, width), BF16),
            jax.ShapeDtypeStruct((4, groups, 16, width // 4), BF16),
        ]
        + rider.shapes,
        scratch_shapes=rider.scratch
        + [
            pltpu.VMEM((length, width), BF16),
            pltpu.VMEM((length, width), F32),
            pltpu.VMEM((groups, 4, part, width), F32),
            pltpu.VMEM((groups, 4, part, width), BF16),
            pltpu.VMEM((groups, 4, part, width), BF16),
            pltpu.SemaphoreType.DMA((groups,)),
            pltpu.SemaphoreType.DMA((groups,)),
        ],
        compiler_params=pltpu.CompilerParams(
            collective_id=rider.call_id, has_side_effects=True, vmem_limit_bytes=60 * 2**20
        ),
        name="tail_back",
    )(grad, y, yr, h, hr, slope, w_out, w_in, adapter, s_act, a_slope, w_do, *rider.inputs)
    return result[:2], result[2:4], result[4:]


def attn_back_kernel(causal, cross, rider, *refs):
    refs = list(refs)

    def take(count):
        got = refs[:count]
        del refs[:count]
        return got

    q_ref, k_ref, kx_ref, v_ref, vx_ref, o_ref, do_ref, lse_ref = take(8)
    if cross:
        wq_ref, wkv_ref, rest_ref, h_ref, hr_ref, w_do_ref = take(6)
    else:
        w_ref, rest_ref = take(2)
    qi_ref, ki_ref = take(2)
    ride_ins = take(len(rider.inputs))
    if cross:
        dpre_ref, do_next_ref, memory_ref = take(3)
    else:
        (dx_ref,) = take(1)
    ride_outs = take(len(rider.inputs))
    ride_sems = take(len(rider.scratch))
    ride = (ride_ins, ride_outs, ride_sems)
    dq_s, own_k, own_v, away_k, away_v, got_k, got_v, acc, send, recv = take(10)
    if cross:
        (acc2,) = take(1)
    step = pl.program_id(0)
    groups = away_k.shape[0]
    width = acc.shape[1]

    def to_sibling(g):
        return [
            remote(a.at[g], b.at[g], send.at[g, j], recv.at[g, j], sibling_of())
            for j, (a, b) in enumerate(((away_k, got_k), (away_v, got_v)))
        ]

    @pl.when(step == 0)
    def _():
        rider.start(*ride)
        acc[...] = rest_ref[...]
        if cross:
            acc2[...] = jnp.zeros_like(acc2)

    @pl.when(step > 0)
    def _():
        g = step - 1
        slot = lax.rem(g, 2)
        for copy in to_sibling(g):
            copy.wait_send()
            copy.wait_recv()
        dk = (own_k[slot] + got_k[g].astype(F32)).astype(BF16)
        dv = (own_v[slot] + got_v[g].astype(F32)).astype(BF16)
        dq = dq_s[slot]
        if cross:
            acc[...] += dot_nt(dq, wq_ref[0])
            acc2[...] += dot_nt(dk, wkv_ref[0, :width]) + dot_nt(dv, wkv_ref[0, width:])
        else:
            acc[...] += (
                dot_nt(dq, w_ref[0, :width])
                + dot_nt(dk, w_ref[0, width : 2 * width])
                + dot_nt(dv, w_ref[0, 2 * width :])
            )

    @pl.when(step < groups)
    def _():
        slot = lax.rem(step, 2)
        attend_back_group(
            (q_ref, (k_ref, kx_ref), (v_ref, vx_ref), o_ref, do_ref, lse_ref),
            (dq_s, slot),
            ((own_k, slot), (away_k, step)),
            ((own_v, slot), (away_v, step)),
            qi_ref,
            ki_ref,
            causal,
        )
        for copy in to_sibling(step):
            copy.start()

    @pl.when(step == groups)
    def _():
        if cross:
            dpre = norm_back_rows(h_ref[...], hr_ref[:, 0:1], acc[...])
            dpre_ref[...] = dpre
            head_grads(dpre.astype(BF16), w_do_ref, do_next_ref)
            memory_ref[...] = acc2[...]
        else:
            dx_ref[...] = acc[...].astype(dx_ref.dtype)
        rider.finish(*ride)


def attn_back(heads, ids, causal, rider, rest, weights, cross=None):
    groups, length, cols = heads[0].shape
    width = rest.shape[1]
    anywhere = pl.BlockSpec(memory_space=pl.ANY)

    def now(shape):
        return pl.BlockSpec((1,) + shape[1:], lambda t: (jnp.minimum(t, groups - 1), 0, 0))

    def past(rows):
        return pl.BlockSpec((1, rows, cols), lambda t: (jnp.maximum(t - 1, 0), 0, 0))

    def whole(v):
        return pl.BlockSpec(v.shape, lambda t: (0,) * len(v.shape))

    wide = jax.ShapeDtypeStruct((length, width), F32)
    if cross:
        h, hr, w_do = cross
        wq, wkv = weights
        extra = [wq, wkv, rest, h, hr, w_do]
        specs = [
            past(width),
            past(2 * width),
            whole(rest),
            whole(h),
            whole(hr),
            pl.BlockSpec((groups, width, cols), lambda t: (0, 3, 0)),
        ]
        outs = [wide, jax.ShapeDtypeStruct(heads[0].shape, BF16), wide]
    else:
        extra = [weights, rest]
        specs = [past(3 * width), whole(rest)]
        outs = [jax.ShapeDtypeStruct((length, width), BF16)]
    moving = pltpu.VMEM((groups, length, cols), BF16)
    result = pl.pallas_call(
        functools.partial(attn_back_kernel, causal, bool(cross), rider),
        grid=(groups + 1,),
        in_specs=[now(v.shape) for v in heads]
        + specs
        + [whole(v) for v in ids]
        + [anywhere] * len(rider.inputs),
        out_specs=[whole(v) for v in outs] + [anywhere] * len(rider.inputs),
        out_shape=outs + rider.shapes,
        scratch_shapes=rider.scratch
        + [
            pltpu.VMEM((2, length, cols), BF16),
            pltpu.VMEM((2, length, cols), F32),
            pltpu.VMEM((2, length, cols), F32),
            moving,
            moving,
            moving,
            moving,
            pltpu.VMEM((length, width), F32),
            pltpu.SemaphoreType.DMA((groups, 2)),
            pltpu.SemaphoreType.DMA((groups, 2)),
        ]
        + ([pltpu.VMEM((length, width), F32)] if cross else []),
        compiler_params=pltpu.CompilerParams(
            collective_id=rider.call_id,
            has_side_effects=True,
            vmem_limit_bytes=60 * 2**20,
        ),
        name="attn_back",
    )(*heads, *extra, *ids, *rider.inputs)
    return result[: len(outs)], result[len(outs) :]


def gather_plain(entry, shards):
    full = [lax.all_gather(lax.all_gather(v, TP), SECTION) for v in shards]
    return [v[entry] for v in full]


def spread(blocks):
    chips = lax.axis_size(CTX) * lax.axis_size(TP)
    kinds, rows, part, width = blocks.shape
    blocks = jnp.pad(blocks, ((0, 0), (0, chips - rows), (0, 0), (0, 0)))
    moved = lax.all_to_all(
        jnp.moveaxis(blocks, 1, 0), (CTX, TP), 0, 0, tiled=True
    )
    return jnp.moveaxis(moved, 0, 1).reshape(kinds, chips * part, width)


def collect(tokens, rows):
    chips = lax.axis_size(CTX) * lax.axis_size(TP)
    kinds, length, width = tokens.shape
    part = length // chips
    blocks = jnp.moveaxis(tokens.reshape(kinds, chips, part, width), 1, 0)
    moved = lax.all_to_all(blocks, (CTX, TP), 0, 0, tiled=True)
    return jnp.moveaxis(moved, 0, 1)[:, :rows]


def per_device(
    layer_inputs,
    out_grad,
    src_seg,
    tgt_seg,
    qkv_weights,
    out_weights,
    cross_weights,
    ffn_in,
    ffn_out,
    adapter_in,
    adapter_in_bias,
    adapter_out,
    adapter_out_bias,
):
    core = lax.axis_index(SECTION)
    is_first = core == 0
    tp = lax.axis_size(TP)
    chips = lax.axis_size(CTX) * tp
    chip = lax.axis_index(CTX) * tp + lax.axis_index(TP)
    _, micro, per_micro, part, width = layer_inputs.shape
    row_count = micro * per_micro
    half = part // 2
    length = half * chips

    def pick(first, second):
        return jnp.where(is_first, first, second)

    x = layer_inputs.reshape(row_count, part, width)
    low, high = x[:, :half], x[:, half:]
    other = swap(pick(high, low))
    grads = out_grad.reshape(row_count, part, width)
    stacked = jnp.stack(
        [pick(low, other), pick(other, high), pick(grads[:, :half], grads[:, half:])]
    )
    near = lax.axis_size(CTX) == 4 and tp == 4
    lanes = adapter_in_bias.shape[1]
    cols = out_weights.shape[2]
    pad = lambda v, n: jnp.pad(v, [(0, n - v.shape[0])] + [(0, 0)] * (v.ndim - 1))
    biases = jnp.concatenate(
        [pad(adapter_in_bias[0], cols)[None], adapter_out_bias[0].reshape(-1, cols)]
    )
    shards = [
        jnp.concatenate([qkv_weights[0], out_weights], axis=0).reshape(-1, cols),
        ffn_in[0],
        ffn_out[0],
        jnp.concatenate(
            [
                jnp.concatenate([adapter_in[0], adapter_out[0].T], axis=1),
                pad(biases, 256),
            ],
            axis=0,
        ),
        cross_weights[0].reshape(-1, cols),
    ]
    if near:
        ids = ids_call(jnp.stack([src_seg, tgt_seg]).reshape(2 * row_count, -1))
        flat_ids = ids.swapaxes(0, 1).reshape(2, row_count, -1)
    else:
        flat_ids = [
            lax.all_gather(v.reshape(row_count, -1), CTX, axis=1, tiled=True)
            for v in (src_seg, tgt_seg)
        ]

    def unpack(full):
        attn, w_in, w_out, adapter, cross = full
        attn = attn.reshape(tp, 4, -1, cols)
        cross = cross.reshape(tp, 2, -1, cols)
        b_out = adapter[0, width + 1 : width + 1 + width // cols].reshape(width)
        tail = (
            w_in,
            w_out,
            adapter[:, :width, :lanes],
            adapter[:, width, :lanes],
            adapter[:, :width, lanes:],
            b_out,
        )
        return attn, cross, tail

    def ids_of(flat):
        row = lax.dynamic_index_in_dim(
            flat, jnp.minimum(chip, row_count - 1), 0, keepdims=False
        )
        return row.reshape(chips, 2, half)

    index = jnp.arange(length, dtype=jnp.int32)
    place = (index // half) * part + index % half

    def cut(seg, which):
        own = lax.dynamic_index_in_dim(seg, which, 1, keepdims=False).reshape(length)
        return own, place + which * half

    src_ids, tgt_ids = ids_of(flat_ids[0]), ids_of(flat_ids[1])

    def id_arrays(seg_q, seg_k):
        qi = jnp.stack(cut(seg_q, core))
        ki = jnp.stack(cut(seg_k, core) + cut(seg_k, 1 - core))
        return (qi.T, ki), (qi, ki.T)

    enc_ids = id_arrays(src_ids, src_ids)
    dec_ids = id_arrays(tgt_ids, tgt_ids)
    cross_ids = id_arrays(tgt_ids, src_ids)

    def scatter(arrays, call_id):
        return Scatter(arrays, row_count, call_id) if near else None

    def tokens(value):
        return value.astype(BF16).reshape(chips, half, width)

    def scatter(arrays, call_id):
        return Scatter(arrays, row_count, call_id) if near else None

    def tokens(value):
        return value.astype(BF16).reshape(chips, half, width)

    if near:
        src_own, place_own = cut(src_ids, core)
        src_oth, place_oth = cut(src_ids, 1 - core)
        tgt_own, tgt_oth = cut(tgt_ids, core)[0], cut(tgt_ids, 1 - core)[0]
        feats = jnp.stack(
            [
                id_columns(src_own, False),
                id_columns(src_own, True),
                id_columns(src_oth, True),
                id_columns(tgt_own, False),
                id_columns(tgt_own, True),
                id_columns(tgt_oth, True),
            ]
        )
        enc_w, dec_w, slope, kept = forward_call(
            shards,
            [stacked[0], stacked[1]],
            place_own[:, None],
            jnp.stack([place_own, place_oth] * 4),
            feats,
        )
        (dec_slope, dec_s, dec_a, dec_y, dec_yr, decoded), (placed,) = tail_call(
            kept[C2],
            (dec_w[1], dec_w[2], dec_w[3]),
            scatter([(stacked[2], Scatter.BRING)], 8),
        )
        cotangent = placed.reshape(length, width)
        encoded_bf = kept[EY].astype(BF16)
    else:
        source, target, cotangent = spread(stacked)
        enc_attn, enc_cross, enc_tail_w = unpack(gather_plain(0, shards))
        dec_attn, dec_cross, dec_tail_w = unpack(gather_plain(1, shards))
        enc_mid, enc_self = self_forward(
            source, source.astype(F32), enc_attn, enc_ids, False
        )
        encoded, enc_tail = tail_forward(enc_mid, enc_tail_w)
        encoded_bf = encoded.astype(BF16)
        memory = [project(encoded_bf, enc_cross[:, j]).astype(BF16) for j in range(2)]
        memory_other = swap(jnp.stack(memory))
        mem_keys = (memory[0], memory_other[0], memory[1], memory_other[1])
        dec_mid, dec_self = self_forward(
            target, target.astype(F32), dec_attn, dec_ids, True
        )
        queries = project(dec_mid.astype(BF16), dec_cross[:, 0]).astype(BF16)
        cross_o, cross_lse = attention_forward(
            queries, mem_keys, cross_ids[0], False
        )
        second, second_rstd = norm(dec_mid + unproject(cross_o, dec_cross[:, 1]))
        decoded, dec_tail = tail_forward(second, dec_tail_w)

    if near:

        def heads(q, k, kx, v, vx, o, lse, do):
            flat = kept[lse].reshape(kept[lse].shape[0], -1, length)
            return [kept[n] for n in (q, k, kx, v, vx, o)] + [do, flat]

        def pieces(parts):
            return [v.reshape((chips,) + v.shape[2:]) for v in parts]

        (grad_cross, do), dec_parts, (out_enc,) = tail_back(
            cotangent,
            dec_y,
            dec_yr,
            kept[C2],
            kept[C2R],
            dec_slope,
            (dec_w[1], dec_w[2], dec_w[3]),
            dec_s,
            dec_a,
            dec_w[4],
            1,
            scatter([(tokens(encoded_bf), 0)], 2),
        )
        (dpre, do, grad_encoded), (out_dec,) = attn_back(
            heads(CQ, MK, MKX, MV, MVX, CO, CL, do),
            cross_ids[1],
            False,
            scatter([(tokens(decoded), 1)], 3),
            grad_cross,
            (dec_w[4], enc_w[4]),
            (kept[DH], kept[DR], dec_w[0]),
        )
        (grad_target,), dec_sum = attn_back(
            heads(DQ, DK, DKX, DV, DVX, DO, DL, do),
            dec_ids[1],
            True,
            scatter([(v, 1) for v in pieces(dec_parts)], 4),
            dpre,
            dec_w[0],
        )
        (dpre, do), enc_parts, (moved,) = tail_back(
            grad_encoded,
            kept[EY],
            kept[EYR],
            kept[EH],
            kept[ER],
            slope,
            (enc_w[1], enc_w[2], enc_w[3]),
            kept[ES],
            kept[EA],
            enc_w[0],
            3,
            scatter([(tokens(grad_target), 1)], 5),
        )
        (grad_source,), enc_sum = attn_back(
            heads(EQ, EK, EKX, EV, EVX, EO, EL, do),
            enc_ids[1],
            False,
            scatter([(v, 0) for v in pieces(enc_parts)], 6),
            dpre,
            enc_w[0],
        )
        outs = pick(out_enc, out_dec)
        sums, ends = [
            jnp.sum(pick(a, b).astype(F32), axis=0) for a, b in zip(enc_sum, dec_sum)
        ]
        part_rows = lanes // 4
        ends = jnp.pad(jnp.sum(ends, axis=0), ((0, 0), (0, width - width // 4)))
        mine = jnp.concatenate([sums.reshape(2 * part_rows, width), ends]).astype(BF16)
        (last,), whole = send_call(scatter([(tokens(grad_source), 0)], 7), mine)
        grads = pick(last, moved).astype(F32)
        whole = whole.astype(F32)
        weights = whole[:, : 2 * part_rows].reshape(4, 2, part_rows, width)
        ends = whole[:, 2 * part_rows :, : width // 4]
        return (
            outs.reshape(layer_inputs.shape),
            grads.reshape(layer_inputs.shape),
            weights[:, 0].reshape(lanes, width).T[None],
            ends[0, 1, :lanes][None],
            weights[:, 1].reshape(1, lanes, width),
            ends[:, 0].reshape(1, width),
        )

    grad_second, dec_terms = tail_backward(cotangent.astype(F32), dec_tail, dec_tail_w)
    grad_cross = norm_back(second, second_rstd, grad_second)
    do = project(grad_cross.astype(BF16), dec_cross[:, 1]).astype(BF16)
    dqc, dmk, dmv = attend_back(
        queries, mem_keys, cross_o, do, cross_lse, cross_ids, False
    )
    grad_first = unproject(dqc, dec_cross[:, 0]) + grad_cross
    grad_target = self_backward(grad_first, dec_self, dec_attn, dec_ids, True)

    grad_encoded = unproject(dmk, enc_cross[:, 0]) + unproject(dmv, enc_cross[:, 1])
    grad_mid, enc_terms = tail_backward(grad_encoded, enc_tail, enc_tail_w)
    grad_source = self_backward(grad_mid, enc_self, enc_attn, enc_ids, False)

    has_row = chip < row_count

    def total(enc_term, dec_term):
        enc_term = jnp.where(has_row, enc_term, 0.0).astype(BF16)
        dec_term = jnp.where(has_row, dec_term, 0.0).astype(BF16)
        got = swap(pick(dec_term, enc_term))
        return (pick(enc_term, dec_term).astype(F32) + got.astype(F32)).astype(BF16)

    sums = [total(e, d) for e, d in zip(enc_terms, dec_terms)]
    scattered = [
        lax.psum_scatter(v, TP, scatter_dimension=0, tiled=False) for v in sums[:3]
    ]
    scattered = [lax.psum(v, CTX).astype(F32) for v in scattered]
    bias_sum = lax.psum(sums[3], (CTX, TP)).astype(F32)

    results = jnp.stack(
        [
            encoded_bf,
            decoded.astype(BF16),
            grad_source.astype(BF16),
            grad_target.astype(BF16),
        ]
    )
    placed = collect(results, row_count)

    def join(enc_part, dec_part):
        mine = pick(enc_part, dec_part)
        got = swap(pick(dec_part, enc_part))
        return jnp.concatenate([pick(mine, got), pick(got, mine)], axis=1)

    outs = join(placed[0], placed[1]).reshape(layer_inputs.shape)
    grads = join(placed[2], placed[3]).astype(F32).reshape(layer_inputs.shape)
    return (
        outs,
        grads,
        scattered[0][None],
        scattered[1][None],
        scattered[2].T[None],
        bias_sum[None],
    )


def solution(mesh):
    return jax.shard_map(
        per_device,
        mesh=mesh,
        in_specs=(
            P(SECTION, None, None, (CTX, TP), None),
            P(None, None, (CTX, TP), None),
            P(None, None, CTX),
            P(None, None, CTX),
            P(SECTION, None, None, TP),
            P(SECTION, None, TP),
            P(SECTION, None, None, TP),
            P(SECTION, None, TP),
            P(SECTION, TP, None),
            P(SECTION, None, TP),
            P(SECTION, TP),
            P(SECTION, TP, None),
            P(SECTION, None),
        ),
        out_specs=(
            P(SECTION, None, None, (CTX, TP), None),
            P(SECTION, None, None, (CTX, TP), None),
            P(SECTION, None, TP),
            P(SECTION, TP),
            P(SECTION, TP, None),
            P(SECTION, None),
        ),
        check_vma=False,
    )
```

profile of v0, /device:TPU:0, one launch (start us, length us, event | category | flops | bytes accessed | tf_op | source)
XLA Modules:
  0.0 619.0 jit_solution(13647472076206624823)
XLA Ops:
  0.7 1.5 broadcast_select_fusion.4
  3.4 7.6 %ids.1 = s32[4,24,256]{2,1,0:T(8,128)} custom-call(s32[24,256]{1,0:T(8,128)} %reshape.727.ids), custom_call_target="tpu_custom_call" | custom-call | tf_op jit(solution)/shard_map/ids/pallas_call | solution.py:1235
  10.9 0.9 fusion.38
  12.7 0.7 fusion.35
  13.9 0.7 fusion.33
  15.2 0.8 fusion.17.refs_7_
  16.4 2.5 pad_maximum_fusion
  20.2 0.7 eq.133
  20.9 1.1 copy.40
  22.0 0.9 copy.43
  22.9 0.9 copy.44
  23.8 0.8 fusion.23.refs_9_
  24.6 2.2 pad_maximum_fusion.1.refs_3_
  26.8 1.0 slice_select_fusion.refs_4_
  27.8 2.5 broadcast_select_fusion.2
  30.3 298.8 %forward.1 = (bf16[4,4096,256]{2,1,0:T(8,128)(2,1)}, bf16[4,1024,1024]{2,1,0:T(8,128)(2,1)}, bf16[4,1024,1024]{2,1,0:T(8,128)(2,1)}, bf16[4,1280,256]{2,1,0:T(8,...) custom-call(bf16[4096,256]{1,0:T(8,128)(2,1)} %bitcast.52, ...), custom_call_target="tpu_custom_call" | custom-call | tf_op jit(solution)/shard_map/forward/pallas_call | solution.py:1174
  329.2 2.7 convert_element_type.86
  331.9 0.6 reshape.733.refs_7_
  333.8 28.9 %tail.1 = (bf16[4,512,1024]{2,1,0:T(8,128)(2,1)}, bf16[4,512,128]{2,1,0:T(8,128)(2,1)}, bf16[4,512,128]{2,1,0:T(8,128)(2,1)}, f32[512,1024]{1,0:T(8,128)}, f32[5...) custom-call(f32[512,1024]{1,0:T(8,128)} %get-tuple-element.77.refs_0_.refs_3_, ...), custom_call_target="tpu_custom_call" | custom-call | tf_op jit(solution)/shard_map/tail/pallas_call | solution.py:1319
  362.7 34.9 %tail_back.2 = (f32[512,1024]{1,0:T(8,128)}, bf16[4,512,256]{2,1,0:T(8,128)(2,1)}, bf16[4,4,32,1024]{3,2,1,0:T(8,128)(2,1)}, bf16[4,4,16,256]{3,2,1,0:T(8,128)(2,1)}, bf16[12,2,32,1024]{3,2,1,0:T(8,128)(2,1)}) custom-call(bf16[512,1024]{1,0:T(8,128)(2,1)} %bitcast.69, f32[512,1024]{1,0:T(8,128)} %get-tuple-element.82.refs_1_, ...), custom_call_target="tpu_custom_call" | custom-call | tf_op jit(solution)/shard_map/tail_back/pallas_call | solution.py:1471
  397.6 55.0 %attn_back.3 = (f32[512,1024]{1,0:T(8,128)}, bf16[4,512,256]{2,1,0:T(8,128)(2,1)}, f32[512,1024]{1,0:T(8,128)}, bf16[12,2,32,1024]{3,2,1,0:T(8,128)(2,1)}) custom-call(bf16[4,512,256]{2,1,0:T(8,128)(2,1)} %get-tuple-element.91.refs_0_, bf16[4,512,256]{2,1,0:T(8,128)(2,1)} %get-tuple-element.92.refs_1_, bf16[4,512,256]{2,1,0:T(8,128)(2,1)} %get-tuple-element.93.refs_2_, ...), custom_call_target="tpu_custom_call" | custom-call | tf_op jit(solution)/shard_map/attn_back/pallas_call | solution.py:1639
  452.6 42.7 %attn_back.4 = (bf16[512,1024]{1,0:T(8,128)(2,1)}, bf16[12,2,32,1024]{3,2,1,0:T(8,128)(2,1)}, bf16[12,2,16,256]{3,2,1,0:T(8,128)(2,1)}) custom-call(bf16[4,512,256]{2,1,0:T(8,128)(2,1)} %get-tuple-element.123.refs_0_, bf16[4,512,256]{2,1,0:T(8,128)(2,1)} %get-tuple-element.124.refs_1_, bf16[4,512,256]{2,1,0:T(8,128)(2,1)} %get-tuple-element.125.refs_2_, ...), custom_call_target="tpu_custom_call" | custom-call | tf_op jit(solution)/shard_map/attn_back/pallas_call | solution.py:1639
  495.3 33.3 %tail_back.3 = (f32[512,1024]{1,0:T(8,128)}, bf16[4,512,256]{2,1,0:T(8,128)(2,1)}, bf16[4,4,32,1024]{3,2,1,0:T(8,128)(2,1)}, bf16[4,4,16,256]{3,2,1,0:T(8,128)(2,1)}, bf16[12,2,32,1024]{3,2,1,0:T(8,128)(2,1)}) custom-call(f32[512,1024]{1,0:T(8,128)} %get-tuple-element.112.refs_0_, f32[512,1024]{1,0:T(8,128)} %get-tuple-element.89.refs_1_, ...), custom_call_target="tpu_custom_call" | custom-call | tf_op jit(solution)/shard_map/tail_back/pallas_call | solution.py:1471
  528.6 52.1 %attn_back.5 = (bf16[512,1024]{1,0:T(8,128)(2,1)}, bf16[12,2,32,1024]{3,2,1,0:T(8,128)(2,1)}, bf16[12,2,16,256]{3,2,1,0:T(8,128)(2,1)}) custom-call(bf16[4,512,256]{2,1,0:T(8,128)(2,1)} %get-tuple-element.106.refs_0_, bf16[4,512,256]{2,1,0:T(8,128)(2,1)} %get-tuple-element.107.refs_1_, bf16[4,512,256]{2,1,0:T(8,128)(2,1)} %get-tuple-element.108.refs_2_, ...), custom_call_target="tpu_custom_call" | custom-call | tf_op jit(solution)/shard_map/attn_back/pallas_call | solution.py:1639
  580.7 1.9 select_reduce_fusion
  582.7 0.7 fusion.21.refs_1_
  583.4 27.3 %send_last.1 = (bf16[12,2,32,1024]{3,2,1,0:T(8,128)(2,1)}, bf16[4,80,1024]{2,1,0:T(8,128)(2,1)}) custom-call(bf16[16,32,1024]{2,1,0:T(8,128)(2,1)} %bitcast.71, bf16[80,1024]{1,0:T(8,128)(2,1)} %fusion.21.refs_1_), custom_call_target="tpu_custom_call" | custom-call | tf_op jit(solution)/shard_map/send_last/pallas_call | solution.py:180
  610.7 1.3 slice.55
  613.1 2.1 convert.14
  615.2 0.9 fusion.37
  616.1 1.0 copy.46
  617.6 1.3 broadcast_select_fusion.1
  (84 shorter events, 7.6 us)
Async XLA Ops:
  0.6 2.1 copy-start.17
  0.6 2.1 copy-start.16
  2.1 13.9 %copy-start.18 = (bf16[1,1024]{1,0:T(2,128)(2,1)S(1)}, bf16[1,1024]{1,0:T(2,128)(2,1)}, u32[]{:S(2)}) copy-start(bf16[1,1024]{1,0:T(2,128)(2,1)} %param.25) | copy-start | bytes 6148
  2.1 13.9 %copy-start.19 = (bf16[1,128]{1,0:T(2,128)(2,1)S(1)}, bf16[1,128]{1,0:T(2,128)(2,1)}, u32[]{:S(2)}) copy-start(bf16[1,128]{1,0:T(2,128)(2,1)} %param.23) | copy-start | bytes 772
  2.1 14.3 %copy-start.6 = (bf16[1,3,1024,256]{3,2,1,0:T(8,128)(2,1)S(1)}, bf16[1,3,1024,256]{3,2,1,0:T(8,128)(2,1)}, u32[]{:S(2)}) copy-start(bf16[1,3,1024,256]{3,2,1,0:T(8,128)(2,1)} %param.17) | copy-start | bytes 4718596
  2.2 25.7 %collective-permute-start = (bf16[12,32,1024]{2,1,0:T(8,128)(2,1)S(1)}, bf16[12,32,1024]{2,1,0:T(8,128)(2,1)}, u32[]{:S(2)}, u32[]{:S(2)}) collective-permute-start(bf16[12,32,1024]{2,1,0:T(8,128)(2,1)S(1)} %broadcast_select_fusion.4), channel_id=1, source_target_pairs={{0,16},{16,0},{1,17},{17,1},{2,18},{18,2},{3,19},{19,3},{4,20},{20... | collective-permute-start | bytes 2359304 | tf_op jit(solution)/shard_map/ppermute | solution.py:20
  2.7 13.7 %copy-start.14 = (s32[128]{0:T(128)}, s32[128]{0:T(128)S(1)}, u32[]{:S(2)}) copy-start(s32[128]{0:T(128)S(1)} %and_select_fusion.2) | copy-start | bytes 1540
  2.7 13.7 %copy-start.15 = (pred[128]{0:T(512)(128)(4,1)}, pred[128]{0:T(512)(128)(4,1)S(1)}, u32[]{:S(2)}) copy-start(pred[128]{0:T(512)(128)(4,1)S(1)} %broadcast_compare_fusion) | copy-start | bytes 388
  19.0 7.9 %copy-start.5 = (bf16[6,2,64,1024]{3,2,1,0:T(8,128)(2,1)S(1)}, bf16[6,2,64,1024]{3,2,1,0:T(8,128)(2,1)}, u32[]{:S(2)}) copy-start(bf16[6,2,64,1024]{3,2,1,0:T(8,128)(2,1)} %param.14) | copy-start | bytes 4718596
  24.6 3.2 copy-start.8
  24.6 3.2 copy-start
  329.1 2.8 copy-start.13
  329.1 3.4 copy-start.12
  329.1 4.0 copy-start.11
  528.6 52.1 %copy-start.7 = (bf16[12,2,32,1024]{3,2,1,0:T(8,128)(2,1)S(1)}, bf16[12,2,32,1024]{3,2,1,0:T(8,128)(2,1)}, u32[]{:S(2)}) copy-start(bf16[12,2,32,1024]{3,2,1,0:T(8,128)(2,1)} %get-tuple-element.142) | copy-start | bytes 4718596
  580.7 1.9 copy-start.9
  580.7 1.9 copy-start.10
  610.7 1.3 copy-start.1
  610.7 2.1 copy-start.3
  610.7 2.2 copy-start.4
  615.2 2.4 copy-start.2
where the time goes:
time: 623 us; the launch traced here: 619 us
  Pallas kernels  581 us (93%)
  other arithmetic  21.8 us (3%)
  local copies, waits for them, and re-layouts  14.9 us (2%)
    pallas_call x1, Pallas kernels, forward_call(): pl.pallas_call(functools.partial(forward_kernel, plan, tokens[0].shape[0]...  299 us
    pallas_call x3, Pallas kernels, attn_back(): pl.pallas_call(functools.partial(attn_back_kernel, causal, bool(cross), r...  150 us
    pallas_call x2, Pallas kernels, tail_back(): pl.pallas_call(functools.partial(tail_back_kernel, rider), grid=(groups +...  68.2 us
    pallas_call x1, Pallas kernels, tail_call(): pl.pallas_call(functools.partial(tail_kernel, rider), grid=(groups + 9,),...  28.9 us
    pallas_call x1, Pallas kernels, send_call(): pl.pallas_call(functools.partial(send_kernel, rider), in_specs=[anywhere]...  27.3 us
  transfers between devices with their start and end apart: 1, of which 0 were waited for; matrix products, arithmetic and copies ran while one was open for 3% of the time, Pallas kernels for 1%

commit v1 on v0

--- a/solution.py
+++ b/solution.py
@@ -269,51 +269,62 @@
     return o, lse.reshape(groups, 2 * pairs, length)
 
 
-def attend_back_group(ins, dq_out, dk_outs, dv_outs, qi_ref, ki_ref, causal):
+def attend_back_group(ins, dq_out, dk_outs, dv_outs, feats, qi_ref, ki_ref, causal):
     q_ref, k_refs, v_refs, o_ref, do_ref, lse_ref = ins
     length = q_ref.shape[1]
-    heads = q_ref.shape[2] // HEAD
     block = length // 2
-    segq = qi_ref[0:1, :]
     posq = qi_ref[1:2, :]
-    ones = jnp.ones((8, HEAD), F32)
-
-    def put(out, rows, cols, value):
-        out[0][out[1], rows, cols] = value.astype(out[0].dtype)
-
-    for h in range(heads):
-        cols = slice(h * HEAD, (h + 1) * HEAD)
-        q_all = q_ref[0, :, cols] * jnp.asarray(SCALE, BF16)
-        do_all = do_ref[0, :, cols]
-        prod = do_all.astype(F32) * o_ref[0, :, cols].astype(F32)
-        delta = dot_nt(ones, prod, precision=lax.Precision.HIGHEST)[0:1]
-        lse = lse_ref[0, h : h + 1, :]
-        dq = [jnp.zeros((block, HEAD), F32), jnp.zeros((block, HEAD), F32)]
+    ones = jnp.ones((8, 2 * HEAD), F32)
+
+    def put(out, rows, lanes, value):
+        out[0][out[1], rows, lanes] = value.astype(out[0].dtype)
+
+    for pair in range(q_ref.shape[2] // (2 * HEAD)):
+        lanes = slice(pair * 2 * HEAD, (pair + 1) * 2 * HEAD)
+        q2 = q_ref[0, :, lanes] * jnp.asarray(SCALE, BF16)
+        do2 = do_ref[0, :, lanes]
+        prod2 = do2.astype(F32) * o_ref[0, :, lanes].astype(F32)
+        dq, dk, dv = [None, None], {}, {}
+        for j in range(2):
+            here = head_mask(length, j)
+            q_all = jnp.where(here, q2, feats[0][...])
+            q_only = jnp.where(here, q2, jnp.zeros_like(q2))
+            do_all = jnp.where(here, do2, jnp.zeros_like(do2))
+            delta = dot_nt(
+                ones, jnp.where(here, prod2, 0.0), precision=lax.Precision.HIGHEST
+            )[0:1]
+            lse = lse_ref[0, 2 * pair + j : 2 * pair + j + 1, :]
+            for n in range(2):
+                for b in range(2):
+                    rows = slice(b * block, (b + 1) * block)
+                    first = b * block if causal else 0
+                    k2 = k_refs[n][0, rows, lanes]
+                    there = head_mask(block, j)
+                    k = jnp.where(there, k2, feats[1 + n][rows])
+                    k_only = jnp.where(there, k2, jnp.zeros_like(k2))
+                    s = dot_nt(k, q_all[first:])
+                    p = jnp.exp(s - lse[:, first:])
+                    if causal:
+                        ok = posq[:, first:] >= ki_ref[rows, 2 * n + 1 : 2 * n + 2]
+                        p = jnp.where(ok, p, 0.0)
+                    dp = dot_nt(v_refs[n][0, rows, lanes], do_all[first:])
+                    ds = (p * (dp - delta[:, first:])).astype(BF16)
+                    add = lambda old, new: new if old is None else old + new
+                    dv[n, b] = add(
+                        dv.get((n, b)), dot_nn(p.astype(BF16), do_all[first:])
+                    )
+                    dk[n, b] = add(dk.get((n, b)), dot_nn(ds, q_only[first:]))
+                    part = dot_tn(k_only, ds)
+                    if not first:
+                        dq[0] = add(dq[0], part[:, :block])
+                    dq[1] = add(dq[1], part[:, block - first :])
         for n in range(2):
-            i = 2 * n
             for b in range(2):
                 rows = slice(b * block, (b + 1) * block)
-                first = b * block if causal else 0
-                q = q_all[first:]
-                do = do_all[first:]
-                k = k_refs[n][0, rows, cols]
-                s = dot_nt(k, q)
-                ok = ki_ref[rows, i : i + 1] == segq[:, first:]
-                if causal:
-                    ok = ok & (posq[:, first:] >= ki_ref[rows, i + 1 : i + 2])
-                p = jnp.where(ok, jnp.exp(s - lse[:, first:]), 0.0)
-                dp = dot_nt(v_refs[n][0, rows, cols], do)
-                ds = (p * (dp - delta[:, first:])).astype(BF16)
-                put(dv_outs[n], rows, cols, dot_nn(p.astype(BF16), do))
-                put(dk_outs[n], rows, cols, dot_nn(ds, q))
-                part = dot_tn(ds, k)
-                if first:
-                    dq[1] = dq[1] + part
-                else:
-                    dq[0] = dq[0] + part[:block]
-                    dq[1] = dq[1] + part[block:]
-        put(dq_out, slice(0, block), cols, dq[0] * SCALE)
-        put(dq_out, slice(block, length), cols, dq[1] * SCALE)
+                put(dv_outs[n], rows, lanes, dv[n, b])
+                put(dk_outs[n], rows, lanes, dk[n, b])
+        for b in range(2):
+            put(dq_out, slice(b * block, (b + 1) * block), lanes, (dq[b] * SCALE).T)
 
 
 def attn_bwd_kernel(
@@ -326,6 +337,9 @@
     o_ref,
     do_ref,
     lse_ref,
+    fq,
+    fo,
+    fx,
     qi_ref,
     ki_ref,
     dq_ref,
@@ -339,16 +353,26 @@
         (dq_ref, 0),
         ((dko_ref, 0), (dkx_ref, 0)),
         ((dvo_ref, 0), (dvx_ref, 0)),
+        (fq, fo, fx),
         qi_ref,
         ki_ref,
         causal,
     )
 
 
+def back_feats(ids):
+    return [
+        id_columns(ids[0][0], False),
+        id_columns(ids[1][:, 0], True),
+        id_columns(ids[1][:, 2], True),
+    ]
+
+
 def attention_backward(q, keys, o, do, lse, ids, causal):
     outs = [jax.ShapeDtypeStruct(q.shape, BF16)] * 5
+    small = [*back_feats(ids), *ids]
     return attention_call(
-        attn_bwd_kernel, "attn_bwd", causal, [q, *keys, o, do, lse], ids, outs
+        attn_bwd_kernel, "attn_bwd", causal, [q, *keys, o, do, lse], small, outs
     )
 
 
@@ -535,21 +559,24 @@
 )
 
 
+LAG = 2
+
+
 def plan_steps(sizes):
     ready, clock = [], 20.0
     for e, g in ORDER:
         for _ in range(3):
-            clock += sizes[g] / 3 * 14e-6
+            clock += sizes[g] / 3 * 11e-6
             ready.append(clock)
-    ticks = len(ready) + 2
-    ready += [clock + 4, clock + 8]
+    ticks = len(ready) + 2 * LAG
+    ready += [clock + 4 * n for n in range(1, 2 * LAG + 1)]
     starts, at, step, now, done = {}, {}, 0, 0.0, 0
     for name, count, need, cost in WORK:
         starts[name] = step
         for n in range(count):
             while done < ticks and (
                 ready[done] <= now
-                or (need and done <= 3 * ORDER.index(need) + 4)
+                or (need and done <= 3 * ORDER.index(need) + 2 + 2 * LAG)
             ):
                 at[done] = step
                 now = max(now, ready[done])
@@ -652,6 +679,7 @@
     (
         z_send,
         z_recv,
+        h_send,
         n_send,
         n_recv,
         f_send,
@@ -678,8 +706,10 @@
     cd = 3 - c
     sib = (1 - s, c, t)
 
+    inner = (t == 1) | (t == 2)
+
     def xor(k):
-        return {1: t + 1 - 2 * lax.rem(t, 2), 2: lax.rem(t + 2, 4), 3: 3 - t}[k]
+        return {1: t + 1 - 2 * lax.rem(t, 2), 2: 2 - t // 2, 3: 3 - 3 * (t // 2)}[k]
 
     def token_copy(kind, i):
         p = lax.rem(chip + i, chips)
@@ -734,7 +764,18 @@
             block(n, t, h, c),
             z_send.at[n, k - 1, h],
             z_recv.at[n, k - 1],
-            (h, c, xor(k)),
+            (h, c, xor(1) if k == 1 else jnp.clip(3 - t, 1, 2)),
+        )
+
+    def z_forward(n, k):
+        src = block(n, xor(k), s, c)
+        to = 3 - t if k == 1 else 3 * t - 3
+        return remote(
+            src,
+            src,
+            h_send.at[n, k - 1],
+            z_recv.at[n, (2, 1, 2)[k - 1]],
+            (s, c, jnp.clip(to, 0, 3)),
         )
 
     def store(g):
@@ -769,8 +810,12 @@
         def _():
             if k == 1:
                 far(n).start()
-            for h in range(2):
-                z_copy(n, k, h).start()
+            if k < 3:
+
+                @pl.when(inner | (k == 1))
+                def _():
+                    for h in range(2):
+                        z_copy(n, k, h).start()
 
     def near_copy(n, k, j):
         src = block(n, xor(k), s, c)
@@ -799,6 +844,7 @@
     def stage2(i):
         n, k = items[i]
         got(block(n, xor(k), s, c), z_recv.at[n, k - 1])
+        pl.when(inner)(z_forward(n, k).start)
         near_copy(n, k, 0).start()
         near_copy(n, k, 1).start()
         sibling_copy(n, k, 0).start()
@@ -836,10 +882,10 @@
             stage2(i)
             if i + window < count:
                 start_z(i + window)
-        if 0 <= i - 1 < count:
-            stage3(i - 1)
-        if 0 <= i - 2 < count:
-            stage4(i - 2)
+        if 0 <= i - LAG < count:
+            stage3(i - LAG)
+        if 0 <= i - 2 * LAG < count:
+            stage4(i - 2 * LAG)
         if i == 3:
             send_tokens(1)
 
@@ -878,7 +924,7 @@
         for i in range(window):
             start_z(i)
 
-    for i in range(count + 2):
+    for i in range(count + 2 * LAG):
         pl.when(step == tick_step[i])(functools.partial(tick, i))
 
     def on(name):
@@ -1118,6 +1164,7 @@
         for g in (FFN_IN, FFN_OUT, ADAPTER):
             arrive(ORDER.index((1, g)))
         for n, k in items:
+            pl.when(inner)(z_forward(n, k).wait_send)
             for j in range(2):
                 near_copy(n, k, j).wait_send()
                 forward_copy(n, k, j).wait_send()
@@ -1128,9 +1175,9 @@
             @pl.when(s == ORDER[n][0])
             def _():
                 far(n).wait_send()
-                for k in (1, 2, 3):
-                    for h in range(2):
-                        z_copy(n, k, h).wait_send()
+                for h in range(2):
+                    z_copy(n, 1, h).wait_send()
+                    pl.when(inner)(z_copy(n, 2, h).wait_send)
 
         for n in KEPT:
             pltpu.make_async_copy(kept[n], kept_out[n], out_sem.at[n]).wait()
@@ -1153,7 +1200,8 @@
     kept = [shapes[kind] for kind in KEPT.values()]
     hidden = shards[FFN_IN].shape[1]
     sizes = [
-        (groups, 3, 2),
+        (groups, 2, 2),
+        (groups, 3),
         (groups, 3),
         (groups, 3, 2),
         (groups, 3, 2),
@@ -1243,6 +1291,9 @@
     )(ids)
 
 
+SPLIT = 1
+
+
 def tail_kernel(rider, *refs):
     refs = list(refs)
 
@@ -1279,7 +1330,7 @@
         a_ref[0] = (sig * (1.0 + pre * (1.0 - sig))).astype(BF16)
         acc[...] += 4.0 * dot_nt(gated, adapter_ref[0, :width, lanes:])
 
-    @pl.when((step >= 4) & (step < 12))
+    @pl.when((step >= 4) & (step < 4 + 4 * SPLIT))
     def _():
         inner = dot_nn(rows_in[...], w_in_ref[0])
         phi = 0.5 * (1.0 + lax.erf(inner * 0.7071067811865476))
@@ -1288,7 +1339,7 @@
         ).astype(BF16)
         acc[...] += dot_nn((inner * phi).astype(BF16), w_out_ref[0])
 
-    @pl.when(step == 12)
+    @pl.when(step == 4 + 4 * SPLIT)
     def _():
         normed, rstd = norm(acc[...])
         y_ref[...] = normed
@@ -1305,8 +1356,8 @@
     anywhere = pl.BlockSpec(memory_space=pl.ANY)
 
     def tile(j):
-        j = jnp.clip(j - groups, 0, 7)
-        return j // 2, lax.rem(j, 2)
+        j = jnp.clip(j - groups, 0, groups * SPLIT - 1)
+        return j // SPLIT, lax.rem(j, SPLIT)
 
     def group(j):
         return jnp.minimum(j, groups - 1)
@@ -1314,15 +1365,15 @@
     wide = pl.BlockSpec((length, width), lambda j: (0, 0))
     gated = pl.BlockSpec((1, length, lanes), lambda j: (group(j), 0, 0))
     cut = lambda rows: pl.BlockSpec(
-        (1, rows, hidden // 2), lambda j: (tile(j)[0], 0, tile(j)[1])
+        (1, rows, hidden // SPLIT), lambda j: (tile(j)[0], 0, tile(j)[1])
     )
     result = pl.pallas_call(
         functools.partial(tail_kernel, rider),
-        grid=(groups + 9,),
+        grid=(groups * (1 + SPLIT) + 1,),
         in_specs=[
             wide,
             cut(width),
-            pl.BlockSpec((1, hidden // 2, width), lambda j: (tile(j)[0], tile(j)[1], 0)),
+            pl.BlockSpec((1, hidden // SPLIT, width), lambda j: (tile(j)[0], tile(j)[1], 0)),
             pl.BlockSpec((1,) + adapter.shape[1:], lambda j: (group(j), 0, 0)),
         ]
         + [anywhere] * len(rider.inputs),
@@ -1429,13 +1480,13 @@
             ).astype(BF16)
         to_sibling(step).start()
 
-    @pl.when((step >= groups) & (step < groups + 8))
+    @pl.when((step >= groups) & (step < groups * (1 + SPLIT)))
     def _():
         dg = dot_nt(db[...], w_out_ref[0])
         df = (dg * slope_ref[0].astype(F32)).astype(BF16)
         acc[...] += dot_nt(df, w_in_ref[0])
 
-    @pl.when(step == groups + 8)
+    @pl.when(step == groups * (1 + SPLIT))
     def _():
         dpre = norm_back_rows(h_ref[...], hr_ref[:, 0:1], acc[...])
         dpre_ref[...] = dpre
@@ -1462,20 +1513,20 @@
         return pl.BlockSpec(v.shape, lambda j: (0, 0))
 
     def tile(j):
-        j = jnp.clip(j - groups, 0, 7)
-        return j // 2, lax.rem(j, 2)
+        j = jnp.clip(j - groups, 0, groups * SPLIT - 1)
+        return j // SPLIT, lax.rem(j, SPLIT)
 
     def group(j):
         return jnp.minimum(j, groups - 1)
 
     result = pl.pallas_call(
         functools.partial(tail_back_kernel, rider),
-        grid=(groups + 9,),
+        grid=(groups * (1 + SPLIT) + 1,),
         in_specs=[whole(v) for v in (grad, y, yr, h, hr)]
         + [
-            pl.BlockSpec((1, length, hidden // 2), lambda j: (tile(j)[0], 0, tile(j)[1])),
-            pl.BlockSpec((1, hidden // 2, width), lambda j: (tile(j)[0], tile(j)[1], 0)),
-            pl.BlockSpec((1, width, hidden // 2), lambda j: (tile(j)[0], 0, tile(j)[1])),
+            pl.BlockSpec((1, length, hidden // SPLIT), lambda j: (tile(j)[0], 0, tile(j)[1])),
+            pl.BlockSpec((1, hidden // SPLIT, width), lambda j: (tile(j)[0], tile(j)[1], 0)),
+            pl.BlockSpec((1, width, hidden // SPLIT), lambda j: (tile(j)[0], 0, tile(j)[1])),
             pl.BlockSpec((1,) + adapter.shape[1:], lambda j: (group(j), 0, 0)),
             pl.BlockSpec((1, length, lanes), lambda j: (group(j), 0, 0)),
             pl.BlockSpec((1, length, lanes), lambda j: (group(j), 0, 0)),
@@ -1527,7 +1578,7 @@
         wq_ref, wkv_ref, rest_ref, h_ref, hr_ref, w_do_ref = take(6)
     else:
         w_ref, rest_ref = take(2)
-    qi_ref, ki_ref = take(2)
+    feats, (qi_ref, ki_ref) = take(3), take(2)
     ride_ins = take(len(rider.inputs))
     if cross:
         dpre_ref, do_next_ref, memory_ref = take(3)
@@ -1584,6 +1635,7 @@
             (dq_s, slot),
             ((own_k, slot), (away_k, step)),
             ((own_v, slot), (away_v, step)),
+            feats,
             qi_ref,
             ki_ref,
             causal,
@@ -1883,7 +1935,7 @@
         )
         (dpre, do, grad_encoded), (out_dec,) = attn_back(
             heads(CQ, MK, MKX, MV, MVX, CO, CL, do),
-            cross_ids[1],
+            [feats[3], feats[1], feats[2], *cross_ids[1]],
             False,
             scatter([(tokens(decoded), 1)], 3),
             grad_cross,
@@ -1892,7 +1944,7 @@
         )
         (grad_target,), dec_sum = attn_back(
             heads(DQ, DK, DKX, DV, DVX, DO, DL, do),
-            dec_ids[1],
+            [feats[3], feats[4], feats[5], *dec_ids[1]],
             True,
             scatter([(v, 1) for v in pieces(dec_parts)], 4),
             dpre,
@@ -1914,7 +1966,7 @@
         )
         (grad_source,), enc_sum = attn_back(
             heads(EQ, EK, EKX, EV, EVX, EO, EL, do),
-            enc_ids[1],
+            [feats[0], feats[1], feats[2], *enc_ids[1]],
             False,
             scatter([(v, 0) for v in pieces(enc_parts)], 6),
             dpre,

time: 623 us -> 583 us (0.936)
  Pallas kernels: 581 us -> 548 us
    pallas_call x1, Pallas kernels: 299 us -> 265 us  [forward_call(): pl.pallas_call(functools.partial(forward_kernel, plan, tokens[0].shape[0]...]
where the time goes in v1:
time: 583 us; the launch traced here: 584 us
  Pallas kernels  548 us (94%)
  other arithmetic  21.3 us (4%)
  local copies, waits for them, and re-layouts  13.4 us (2%)
    pallas_call x1, Pallas kernels, forward_call(): pl.pallas_call(functools.partial(forward_kernel, plan, tokens[0].shape[0]...  265 us
    pallas_call x3, Pallas kernels, attn_back(): pl.pallas_call(functools.partial(attn_back_kernel, causal, bool(cross), r...  152 us
    pallas_call x2, Pallas kernels, tail_back(): pl.pallas_call(functools.partial(tail_back_kernel, rider), grid=(groups *...  68.1 us
    pallas_call x1, Pallas kernels, tail_call(): pl.pallas_call(functools.partial(tail_kernel, rider), grid=(groups * (1 +...  27.8 us
    pallas_call x1, Pallas kernels, send_call(): pl.pallas_call(functools.partial(send_kernel, rider), in_specs=[anywhere]...  27.3 us
  transfers between devices with their start and end apart: 1, of which 0 were waited for; matrix products, arithmetic and copies ran while one was open for 3% of the time, Pallas kernels for 1%

profile of v1, /device:TPU:0, one launch (start us, length us, event | category | flops | bytes accessed | tf_op | source)
XLA Modules:
  0.0 584.3 jit_solution(2449284353333634248)
XLA Ops:
  0.7 1.5 broadcast_select_fusion.4
  3.3 7.6 %ids.1 = s32[4,24,256]{2,1,0:T(8,128)} custom-call(s32[24,256]{1,0:T(8,128)} %reshape.727.ids), custom_call_target="tpu_custom_call" | custom-call | tf_op jit(solution)/shard_map/ids/pallas_call | solution.py:1283
  10.9 0.9 fusion.46
  12.7 0.7 fusion.43
  13.9 0.7 fusion.41
  15.3 0.8 fusion.25.refs_7_
  16.6 2.8 pad_maximum_fusion
  20.9 0.9 copy.43
  21.8 0.9 copy.44
  22.7 1.2 fusion.22
  23.9 0.9 pad_maximum_fusion.1.refs_3_
  24.8 1.0 slice_select_fusion.refs_4_
  25.8 2.5 broadcast_select_fusion.2
  28.3 264.9 %forward.1 = (bf16[4,4096,256]{2,1,0:T(8,128)(2,1)}, bf16[4,1024,1024]{2,1,0:T(8,128)(2,1)}, bf16[4,1024,1024]{2,1,0:T(8,128)(2,1)}, bf16[4,1280,256]{2,1,0:T(8,...) custom-call(bf16[4096,256]{1,0:T(8,128)(2,1)} %bitcast.52, ...), custom_call_target="tpu_custom_call" | custom-call | tf_op jit(solution)/shard_map/forward/pallas_call | solution.py:1222
  293.2 2.7 convert_element_type.56
  295.9 0.6 reshape.733.refs_7_
  296.6 0.6 reshape.736.refs_7_
  297.2 0.6 reshape.740.refs_7_
  297.9 27.8 %tail.1 = (bf16[4,512,1024]{2,1,0:T(8,128)(2,1)}, bf16[4,512,128]{2,1,0:T(8,128)(2,1)}, bf16[4,512,128]{2,1,0:T(8,128)(2,1)}, f32[512,1024]{1,0:T(8,128)}, f32[5...) custom-call(f32[512,1024]{1,0:T(8,128)} %get-tuple-element.77.refs_0_.refs_3_, ...), custom_call_target="tpu_custom_call" | custom-call | tf_op jit(solution)/shard_map/tail/pallas_call | solution.py:1370
  325.7 36.5 %tail_back.2 = (f32[512,1024]{1,0:T(8,128)}, bf16[4,512,256]{2,1,0:T(8,128)(2,1)}, bf16[4,4,32,1024]{3,2,1,0:T(8,128)(2,1)}, bf16[4,4,16,256]{3,2,1,0:T(8,128)(2,1)}, bf16[12,2,32,1024]{3,2,1,0:T(8,128)(2,1)}) custom-call(bf16[512,1024]{1,0:T(8,128)(2,1)} %bitcast.69, f32[512,1024]{1,0:T(8,128)} %get-tuple-element.82.refs_1_, ...), custom_call_target="tpu_custom_call" | custom-call | tf_op jit(solution)/shard_map/tail_back/pallas_call | solution.py:1522
  362.2 55.0 %attn_back.3 = (f32[512,1024]{1,0:T(8,128)}, bf16[4,512,256]{2,1,0:T(8,128)(2,1)}, f32[512,1024]{1,0:T(8,128)}, bf16[12,2,32,1024]{3,2,1,0:T(8,128)(2,1)}) custom-call(bf16[4,512,256]{2,1,0:T(8,128)(2,1)} %get-tuple-element.91.refs_0_, bf16[4,512,256]{2,1,0:T(8,128)(2,1)} %get-tuple-element.92.refs_1_, bf16[4,512,256]{2,1,0:T(8,128)(2,1)} %get-tuple-element.93.refs_2_, ...), custom_call_target="tpu_custom_call" | custom-call | tf_op jit(solution)/shard_map/attn_back/pallas_call | solution.py:1691
  417.2 42.9 %attn_back.4 = (bf16[512,1024]{1,0:T(8,128)(2,1)}, bf16[12,2,32,1024]{3,2,1,0:T(8,128)(2,1)}, bf16[12,2,16,256]{3,2,1,0:T(8,128)(2,1)}) custom-call(bf16[4,512,256]{2,1,0:T(8,128)(2,1)} %get-tuple-element.123.refs_0_, bf16[4,512,256]{2,1,0:T(8,128)(2,1)} %get-tuple-element.124.refs_1_, bf16[4,512,256]{2,1,0:T(8,128)(2,1)} %get-tuple-element.125.refs_2_, ...), custom_call_target="tpu_custom_call" | custom-call | tf_op jit(solution)/shard_map/attn_back/pallas_call | solution.py:1691
  460.1 31.6 %tail_back.3 = (f32[512,1024]{1,0:T(8,128)}, bf16[4,512,256]{2,1,0:T(8,128)(2,1)}, bf16[4,4,32,1024]{3,2,1,0:T(8,128)(2,1)}, bf16[4,4,16,256]{3,2,1,0:T(8,128)(2,1)}, bf16[12,2,32,1024]{3,2,1,0:T(8,128)(2,1)}) custom-call(f32[512,1024]{1,0:T(8,128)} %get-tuple-element.112.refs_0_, f32[512,1024]{1,0:T(8,128)} %get-tuple-element.89.refs_1_, ...), custom_call_target="tpu_custom_call" | custom-call | tf_op jit(solution)/shard_map/tail_back/pallas_call | solution.py:1522
  491.7 54.2 %attn_back.5 = (bf16[512,1024]{1,0:T(8,128)(2,1)}, bf16[12,2,32,1024]{3,2,1,0:T(8,128)(2,1)}, bf16[12,2,16,256]{3,2,1,0:T(8,128)(2,1)}) custom-call(bf16[4,512,256]{2,1,0:T(8,128)(2,1)} %get-tuple-element.106.refs_0_, bf16[4,512,256]{2,1,0:T(8,128)(2,1)} %get-tuple-element.107.refs_1_, bf16[4,512,256]{2,1,0:T(8,128)(2,1)} %get-tuple-element.108.refs_2_, ...), custom_call_target="tpu_custom_call" | custom-call | tf_op jit(solution)/shard_map/attn_back/pallas_call | solution.py:1691
  545.9 1.9 select_reduce_fusion
  547.9 0.7 fusion.29.refs_1_
  548.6 27.3 %send_last.1 = (bf16[12,2,32,1024]{3,2,1,0:T(8,128)(2,1)}, bf16[4,80,1024]{2,1,0:T(8,128)(2,1)}) custom-call(bf16[16,32,1024]{2,1,0:T(8,128)(2,1)} %bitcast.71, bf16[80,1024]{1,0:T(8,128)(2,1)} %fusion.29.refs_1_), custom_call_target="tpu_custom_call" | custom-call | tf_op jit(solution)/shard_map/send_last/pallas_call | solution.py:180
  575.9 1.3 slice.55
  578.3 2.1 convert.14
  580.3 0.9 fusion.45
  581.2 1.0 copy.46
  582.7 1.3 broadcast_select_fusion.1
  (85 shorter events, 6.8 us)
Async XLA Ops:
  0.6 2.1 copy-start.17
  0.6 2.1 copy-start.16
  2.1 13.9 %copy-start.18 = (bf16[1,1024]{1,0:T(2,128)(2,1)S(1)}, bf16[1,1024]{1,0:T(2,128)(2,1)}, u32[]{:S(2)}) copy-start(bf16[1,1024]{1,0:T(2,128)(2,1)} %param.25) | copy-start | bytes 6148
  2.1 14.0 %copy-start.19 = (bf16[1,128]{1,0:T(2,128)(2,1)S(1)}, bf16[1,128]{1,0:T(2,128)(2,1)}, u32[]{:S(2)}) copy-start(bf16[1,128]{1,0:T(2,128)(2,1)} %param.23) | copy-start | bytes 772
  2.1 14.5 %copy-start.6 = (bf16[1,3,1024,256]{3,2,1,0:T(8,128)(2,1)S(1)}, bf16[1,3,1024,256]{3,2,1,0:T(8,128)(2,1)}, u32[]{:S(2)}) copy-start(bf16[1,3,1024,256]{3,2,1,0:T(8,128)(2,1)} %param.17) | copy-start | bytes 4718596
  2.2 23.7 %collective-permute-start = (bf16[12,32,1024]{2,1,0:T(8,128)(2,1)S(1)}, bf16[12,32,1024]{2,1,0:T(8,128)(2,1)}, u32[]{:S(2)}, u32[]{:S(2)}) collective-permute-start(bf16[12,32,1024]{2,1,0:T(8,128)(2,1)S(1)} %broadcast_select_fusion.4), channel_id=1, source_target_pairs={{0,16},{16,0},{1,17},{17,1},{2,18},{18,2},{3,19},{19,3},{4,20},{20... | collective-permute-start | bytes 2359304 | tf_op jit(solution)/shard_map/ppermute | solution.py:20
  16.6 2.9 copy-start.8
  16.6 4.1 copy-start.10
  19.5 4.4 copy-start.9
  20.8 4.1 copy-start.5
  23.9 1.9 copy-start
  293.2 2.8 copy-start.15
  293.2 3.4 copy-start.14
  293.2 4.0 copy-start.13
  491.7 54.2 %copy-start.7 = (bf16[12,2,32,1024]{3,2,1,0:T(8,128)(2,1)S(1)}, bf16[12,2,32,1024]{3,2,1,0:T(8,128)(2,1)}, u32[]{:S(2)}) copy-start(bf16[12,2,32,1024]{3,2,1,0:T(8,128)(2,1)} %get-tuple-element.142) | copy-start | bytes 4718596
  545.9 1.9 copy-start.11
  545.9 1.9 copy-start.12
  575.9 1.3 copy-start.1
  575.9 2.1 copy-start.3
  575.9 2.2 copy-start.4
  580.3 2.4 copy-start.2

commit v2 on v1

--- a/solution.py
+++ b/solution.py
@@ -274,7 +274,7 @@
     length = q_ref.shape[1]
     block = length // 2
     posq = qi_ref[1:2, :]
-    ones = jnp.ones((8, 2 * HEAD), F32)
+    ones = jnp.ones((16, 2 * HEAD), BF16)
 
     def put(out, rows, lanes, value):
         out[0][out[1], rows, lanes] = value.astype(out[0].dtype)
@@ -290,9 +290,10 @@
             q_all = jnp.where(here, q2, feats[0][...])
             q_only = jnp.where(here, q2, jnp.zeros_like(q2))
             do_all = jnp.where(here, do2, jnp.zeros_like(do2))
-            delta = dot_nt(
-                ones, jnp.where(here, prod2, 0.0), precision=lax.Precision.HIGHEST
-            )[0:1]
+            prod = jnp.where(here, prod2, 0.0)
+            high = prod.astype(BF16)
+            rest = (prod - high.astype(F32)).astype(BF16)
+            delta = (dot_nt(ones, high) + dot_nt(ones, rest))[0:1]
             lse = lse_ref[0, 2 * pair + j : 2 * pair + j + 1, :]
             for n in range(2):
                 for b in range(2):
@@ -667,7 +668,7 @@
         return got
 
     shards = take(5)
-    tokens = take(2)
+    (tokens,) = take(1)
     col_ref, row_ref, feat_ref = take(3)
     full = (take(5), take(5))
     (slope_out,) = take(1)
@@ -711,36 +712,49 @@
     def xor(k):
         return {1: t + 1 - 2 * lax.rem(t, 2), 2: 2 - t // 2, 3: 3 - 3 * (t // 2)}[k]
 
-    def token_copy(kind, i):
+    part = xs[0].shape[1]
+
+    def token_copy(kind, i, h):
         p = lax.rem(chip + i, chips)
-        src = tokens[kind].at[jnp.minimum(p, rows - 1)]
+        src = tokens.at[jnp.minimum(p, rows - 1), pl.ds(h * part, part)]
         dst = xs[kind].at[chip]
-        if i == 0:
-            return p, pltpu.make_async_copy(src, dst, t_send.at[kind, 0])
+        if i == 0 and h == kind:
+            return p, pltpu.make_async_copy(src, dst, t_send.at[kind, 0, h])
         return p, remote(
-            src, dst, t_send.at[kind, i], t_recv.at[kind, i], device_of(s, p)
+            src, dst, t_send.at[kind, i, h], t_recv.at[kind, i], device_of(h, p)
         )
 
     def send_tokens(kind):
-        for i in range(chips):
-            p, copy = token_copy(kind, i)
-            pl.when(p < rows)(copy.start)
+        @pl.when(s == kind)
+        def _():
+            for i in range(chips):
+                for h in range(2):
+                    p, copy = token_copy(kind, i, h)
+                    pl.when(p < rows)(copy.start)
 
     def got(region, sem):
         remote(region, region, load_sem.at[0], sem, sib).wait_recv()
 
     def wait_tokens(kind):
-        for i in range(chips):
-            p, copy = token_copy(kind, i)
-            pl.when(p < rows)(copy.wait if i == 0 else copy.wait_send)
-            if i:
-
-                @pl.when(chip < rows)
-                def _():
-                    got(
-                        xs[kind].at[lax.rem(chip + chips - i, chips)],
-                        t_recv.at[kind, i],
-                    )
+        @pl.when(s == kind)
+        def _():
+            for i in range(chips):
+                for h in range(2):
+                    p, copy = token_copy(kind, i, h)
+                    stays = i == 0 and h == kind
+                    pl.when(p < rows)(copy.wait if stays else copy.wait_send)
+
+        @pl.when(chip < rows)
+        def _():
+            for i in range(chips):
+                region = xs[kind].at[lax.rem(chip + chips - i, chips)]
+                if i:
+                    got(region, t_recv.at[kind, i])
+                else:
+
+                    @pl.when(s != kind)
+                    def _():
+                        got(region, t_recv.at[kind, 0])
 
     items = [(n, k) for n in range(len(ORDER)) for k in (1, 2, 3)]
     window = 4
@@ -1184,7 +1198,8 @@
 
 
 def forward_call(shards, tokens, col, row, feats):
-    part, width = tokens[0].shape[1:]
+    rows, part, width = tokens.shape
+    part //= 2
     length = 16 * part
     groups = len(ORDER)
     dma = pltpu.SemaphoreType.DMA
@@ -1210,7 +1225,7 @@
         (groups, 3, 4),
         (groups, 3, 4),
         (groups, 4),
-        (2, 16),
+        (2, 16, 2),
         (2, 16),
         (3, 4, 2),
         (3, 4, 2),
@@ -1220,9 +1235,9 @@
     ]
     plan = plan_steps([v.size * 2 for v in shards])
     result = pl.pallas_call(
-        functools.partial(forward_kernel, plan, tokens[0].shape[0]),
+        functools.partial(forward_kernel, plan, rows),
         grid=(plan[2],),
-        in_specs=[anywhere] * 7
+        in_specs=[anywhere] * 6
         + [
             pl.BlockSpec(col.shape, lambda i: (0, 0)),
             pl.BlockSpec(row.shape, lambda i: (0, 0)),
@@ -1248,7 +1263,7 @@
             collective_id=0, has_side_effects=True, vmem_limit_bytes=60 * 2**20
         ),
         name="forward",
-    )(*shards, *tokens, col, row, feats)
+    )(*shards, tokens, col, row, feats)
     return result[:5], result[5:10], result[10], result[11:]
 
 
@@ -1454,39 +1469,49 @@
         acc[...] = dpre
         db[...] = dpre.astype(BF16)
 
-    @pl.when(step < groups)
+    @pl.when(step == 0)
     def _():
         branch = db[...]
-        ds = 4.0 * dot_nn(branch, adapter_ref[0, :width, lanes:])
-        du = (ds * a_ref[0].astype(F32)).astype(BF16)
-        acc[...] += dot_nt(du, adapter_ref[0, :width, :lanes])
-        d_in = dot_tn(du, h_ref[...].astype(BF16))
-        d_out = 4.0 * dot_tn(s_ref[0], branch)
+        rows_in = h_ref[...].astype(BF16)
+        beside = lambda r: jnp.concatenate([r[g] for g in range(groups)], axis=1)
+        a_in = jnp.concatenate(
+            [adapter_ref[g, :width, :lanes] for g in range(groups)], axis=1
+        )
+        a_out = jnp.concatenate(
+            [adapter_ref[g, :width, lanes:] for g in range(groups)], axis=1
+        )
+        ds = 4.0 * dot_nn(branch, a_out)
+        du = (ds * beside(a_ref).astype(F32)).astype(BF16)
+        acc[...] += dot_nt(du, a_in)
+        d_in = dot_tn(du, rows_in)
+        d_out = 4.0 * dot_tn(beside(s_ref), branch)
         last = 4.0 * jnp.sum(branch.astype(F32), axis=0, keepdims=True)
         bias = jnp.sum(du.astype(F32), axis=0, keepdims=True)
         cut = width // 4
-        bias = jnp.concatenate([bias, jnp.zeros((1, cut - lanes), F32)], axis=1)
+        blank = jnp.zeros((1, cut - lanes), F32)
         row = lax.broadcasted_iota(jnp.int32, (16, cut), 0)
         part = lanes // 4
-        for c in range(4):
-            one = d_in[c * part : (c + 1) * part]
-            two = d_out[c * part : (c + 1) * part]
-            mine[step, c] = jnp.where(first, one, two)
-            away[step, c] = jnp.where(first, two, one).astype(BF16)
-            tails_ref[c, step] = jnp.where(
-                row == 0,
-                last[:, c * cut : (c + 1) * cut],
-                jnp.where(row == 1, bias, 0.0),
-            ).astype(BF16)
-        to_sibling(step).start()
-
-    @pl.when((step >= groups) & (step < groups * (1 + SPLIT)))
+        for g in range(groups):
+            own = bias[:, g * lanes : (g + 1) * lanes]
+            second = jnp.where(row == 1, jnp.concatenate([own, blank], axis=1), 0.0)
+            for c in range(4):
+                start = g * lanes + c * part
+                one = d_in[start : start + part]
+                two = d_out[start : start + part]
+                mine[g, c] = jnp.where(first, one, two)
+                away[g, c] = jnp.where(first, two, one).astype(BF16)
+                tails_ref[c, g] = jnp.where(
+                    row == 0, last[:, c * cut : (c + 1) * cut], second
+                ).astype(BF16)
+            to_sibling(g).start()
+
+    @pl.when((step >= 1) & (step < 1 + groups * SPLIT))
     def _():
         dg = dot_nt(db[...], w_out_ref[0])
         df = (dg * slope_ref[0].astype(F32)).astype(BF16)
         acc[...] += dot_nt(df, w_in_ref[0])
 
-    @pl.when(step == groups * (1 + SPLIT))
+    @pl.when(step == 1 + groups * SPLIT)
     def _():
         dpre = norm_back_rows(h_ref[...], hr_ref[:, 0:1], acc[...])
         dpre_ref[...] = dpre
@@ -1513,23 +1538,20 @@
         return pl.BlockSpec(v.shape, lambda j: (0, 0))
 
     def tile(j):
-        j = jnp.clip(j - groups, 0, groups * SPLIT - 1)
+        j = jnp.clip(j - 1, 0, groups * SPLIT - 1)
         return j // SPLIT, lax.rem(j, SPLIT)
-
-    def group(j):
-        return jnp.minimum(j, groups - 1)
 
     result = pl.pallas_call(
         functools.partial(tail_back_kernel, rider),
-        grid=(groups * (1 + SPLIT) + 1,),
+        grid=(groups * SPLIT + 2,),
         in_specs=[whole(v) for v in (grad, y, yr, h, hr)]
         + [
             pl.BlockSpec((1, length, hidden // SPLIT), lambda j: (tile(j)[0], 0, tile(j)[1])),
             pl.BlockSpec((1, hidden // SPLIT, width), lambda j: (tile(j)[0], tile(j)[1], 0)),
             pl.BlockSpec((1, width, hidden // SPLIT), lambda j: (tile(j)[0], 0, tile(j)[1])),
-            pl.BlockSpec((1,) + adapter.shape[1:], lambda j: (group(j), 0, 0)),
-            pl.BlockSpec((1, length, lanes), lambda j: (group(j), 0, 0)),
-            pl.BlockSpec((1, length, lanes), lambda j: (group(j), 0, 0)),
+            pl.BlockSpec(adapter.shape, lambda j: (0, 0, 0)),
+            pl.BlockSpec((groups, length, lanes), lambda j: (0, 0, 0)),
+            pl.BlockSpec((groups, length, lanes), lambda j: (0, 0, 0)),
             pl.BlockSpec((groups, width, cols), lambda j: (0, do_block, 0)),
         ]
         + [anywhere] * len(rider.inputs),
@@ -1774,12 +1796,8 @@
         return jnp.where(is_first, first, second)
 
     x = layer_inputs.reshape(row_count, part, width)
-    low, high = x[:, :half], x[:, half:]
-    other = swap(pick(high, low))
     grads = out_grad.reshape(row_count, part, width)
-    stacked = jnp.stack(
-        [pick(low, other), pick(other, high), pick(grads[:, :half], grads[:, half:])]
-    )
+    grads = pick(grads[:, :half], grads[:, half:])
     near = lax.axis_size(CTX) == 4 and tp == 4
     lanes = adapter_in_bias.shape[1]
     cols = out_weights.shape[2]
@@ -1876,7 +1894,7 @@
         )
         enc_w, dec_w, slope, kept = forward_call(
             shards,
-            [stacked[0], stacked[1]],
+            x,
             place_own[:, None],
             jnp.stack([place_own, place_oth] * 4),
             feats,
@@ -1884,12 +1902,16 @@
         (dec_slope, dec_s, dec_a, dec_y, dec_yr, decoded), (placed,) = tail_call(
             kept[C2],
             (dec_w[1], dec_w[2], dec_w[3]),
-            scatter([(stacked[2], Scatter.BRING)], 8),
+            scatter([(grads, Scatter.BRING)], 8),
         )
         cotangent = placed.reshape(length, width)
         encoded_bf = kept[EY].astype(BF16)
     else:
-        source, target, cotangent = spread(stacked)
+        low, high = x[:, :half], x[:, half:]
+        other = swap(pick(high, low))
+        source, target, cotangent = spread(
+            jnp.stack([pick(low, other), pick(other, high), grads])
+        )
         enc_attn, enc_cross, enc_tail_w = unpack(gather_plain(0, shards))
         dec_attn, dec_cross, dec_tail_w = unpack(gather_plain(1, shards))
         enc_mid, enc_self = self_forward(

time: 583 us -> 576 us (0.988); the launches traced: 584 us -> 567 us
  Pallas kernels: 548 us -> 537 us
  transfers between devices with their start and end apart: 1 -> 0, of which waited for: 0 -> 0; matrix products, arithmetic and copies ran while one was open for 3% -> 0% of each run, Pallas kernels for 1% -> 0%
where the time goes in v2:
time: 576 us; the launch traced here: 567 us
  Pallas kernels  537 us (93%)
  other arithmetic  16.7 us (3%)
  local copies, waits for them, and re-layouts  12.2 us (2%)
    pallas_call x1, Pallas kernels, forward_call(): pl.pallas_call(functools.partial(forward_kernel, plan, rows), grid=(plan[...  260 us
    pallas_call x3, Pallas kernels, attn_back(): pl.pallas_call(functools.partial(attn_back_kernel, causal, bool(cross), r...  146 us
    pallas_call x2, Pallas kernels, tail_back(): pl.pallas_call(functools.partial(tail_back_kernel, rider), grid=(groups *...  68.5 us
    pallas_call x1, Pallas kernels, send_call(): pl.pallas_call(functools.partial(send_kernel, rider), in_specs=[anywhere]...  27.3 us
    pallas_call x1, Pallas kernels, tail_call(): pl.pallas_call(functools.partial(tail_kernel, rider), grid=(groups * (1 +...  26.9 us

profile of v2, /device:TPU:0, one launch (start us, length us, event | category | flops | bytes accessed | tf_op | source)
XLA Modules:
  0.0 567.5 jit_solution(16720472538567317058)
XLA Ops:
  0.7 0.9 pad_add_fusion
  2.2 7.9 %ids.1 = s32[4,24,256]{2,1,0:T(8,128)} custom-call(s32[24,256]{1,0:T(8,128)} %reshape.727.ids), custom_call_target="tpu_custom_call" | custom-call | tf_op jit(solution)/shard_map/ids/pallas_call | solution.py:1298
  10.1 0.9 fusion.46
  11.9 0.7 fusion.43
  13.3 0.7 fusion.41
  14.7 0.7 stack.18.refs_7_
  15.4 0.8 fusion.25.refs_6_
  16.2 1.5 pad_maximum_fusion
  18.0 0.9 pad_maximum_fusion.1.refs_3_
  18.9 260.4 %forward.1 = (bf16[4,4096,256]{2,1,0:T(8,128)(2,1)}, bf16[4,1024,1024]{2,1,0:T(8,128)(2,1)}, bf16[4,1024,1024]{2,1,0:T(8,128)(2,1)}, bf16[4,1280,256]{2,1,0:T(8,...) custom-call(bf16[4096,256]{1,0:T(8,128)(2,1)} %bitcast.52, ...), custom_call_target="tpu_custom_call" | custom-call | tf_op jit(solution)/shard_map/forward/pallas_call | solution.py:1237
  279.3 1.0 slice_select_fusion.refs_4_
  280.3 26.9 %tail.1 = (bf16[4,512,1024]{2,1,0:T(8,128)(2,1)}, bf16[4,512,128]{2,1,0:T(8,128)(2,1)}, bf16[4,512,128]{2,1,0:T(8,128)(2,1)}, f32[512,1024]{1,0:T(8,128)}, f32[5...) custom-call(f32[512,1024]{1,0:T(8,128)} %get-tuple-element.77.refs_0_.refs_3_, ...), custom_call_target="tpu_custom_call" | custom-call | tf_op jit(solution)/shard_map/tail/pallas_call | solution.py:1385
  307.2 1.1 convert_element_type.56
  308.4 37.4 %tail_back.2 = (f32[512,1024]{1,0:T(8,128)}, bf16[4,512,256]{2,1,0:T(8,128)(2,1)}, bf16[4,4,32,1024]{3,2,1,0:T(8,128)(2,1)}, bf16[4,4,16,256]{3,2,1,0:T(8,128)(2,1)}, bf16[12,2,32,1024]{3,2,1,0:T(8,128)(2,1)}) custom-call(bf16[512,1024]{1,0:T(8,128)(2,1)} %bitcast.68, f32[512,1024]{1,0:T(8,128)} %get-tuple-element.82.refs_1_, ...), custom_call_target="tpu_custom_call" | custom-call | tf_op jit(solution)/shard_map/tail_back/pallas_call | solution.py:1544
  345.8 0.6 reshape.733.refs_7_
  346.4 1.2 fusion.22
  347.9 0.9 copy.43
  349.4 51.8 %attn_back.3 = (f32[512,1024]{1,0:T(8,128)}, bf16[4,512,256]{2,1,0:T(8,128)(2,1)}, f32[512,1024]{1,0:T(8,128)}, bf16[12,2,32,1024]{3,2,1,0:T(8,128)(2,1)}) custom-call(bf16[4,512,256]{2,1,0:T(8,128)(2,1)} %get-tuple-element.91.refs_0_, bf16[4,512,256]{2,1,0:T(8,128)(2,1)} %get-tuple-element.92.refs_1_, bf16[4,512,256]{2,1,0:T(8,128)(2,1)} %get-tuple-element.93.refs_2_, ...), custom_call_target="tpu_custom_call" | custom-call | tf_op jit(solution)/shard_map/attn_back/pallas_call | solution.py:1713
  401.2 0.6 reshape.736.refs_7_
  401.9 0.9 copy.44
  402.7 40.8 %attn_back.4 = (bf16[512,1024]{1,0:T(8,128)(2,1)}, bf16[12,2,32,1024]{3,2,1,0:T(8,128)(2,1)}, bf16[12,2,16,256]{3,2,1,0:T(8,128)(2,1)}) custom-call(bf16[4,512,256]{2,1,0:T(8,128)(2,1)} %get-tuple-element.123.refs_0_, bf16[4,512,256]{2,1,0:T(8,128)(2,1)} %get-tuple-element.124.refs_1_, bf16[4,512,256]{2,1,0:T(8,128)(2,1)} %get-tuple-element.125.refs_2_, ...), custom_call_target="tpu_custom_call" | custom-call | tf_op jit(solution)/shard_map/attn_back/pallas_call | solution.py:1713
  443.5 31.1 %tail_back.3 = (f32[512,1024]{1,0:T(8,128)}, bf16[4,512,256]{2,1,0:T(8,128)(2,1)}, bf16[4,4,32,1024]{3,2,1,0:T(8,128)(2,1)}, bf16[4,4,16,256]{3,2,1,0:T(8,128)(2,1)}, bf16[12,2,32,1024]{3,2,1,0:T(8,128)(2,1)}) custom-call(f32[512,1024]{1,0:T(8,128)} %get-tuple-element.112.refs_0_, f32[512,1024]{1,0:T(8,128)} %get-tuple-element.89.refs_1_, ...), custom_call_target="tpu_custom_call" | custom-call | tf_op jit(solution)/shard_map/tail_back/pallas_call | solution.py:1544
  474.7 0.6 reshape.740.refs_7_
  475.4 53.7 %attn_back.5 = (bf16[512,1024]{1,0:T(8,128)(2,1)}, bf16[12,2,32,1024]{3,2,1,0:T(8,128)(2,1)}, bf16[12,2,16,256]{3,2,1,0:T(8,128)(2,1)}) custom-call(bf16[4,512,256]{2,1,0:T(8,128)(2,1)} %get-tuple-element.106.refs_0_, bf16[4,512,256]{2,1,0:T(8,128)(2,1)} %get-tuple-element.107.refs_1_, bf16[4,512,256]{2,1,0:T(8,128)(2,1)} %get-tuple-element.108.refs_2_, ...), custom_call_target="tpu_custom_call" | custom-call | tf_op jit(solution)/shard_map/attn_back/pallas_call | solution.py:1713
  529.1 1.9 select_reduce_fusion
  531.1 0.7 fusion.29.refs_1_
  531.8 27.3 %send_last.1 = (bf16[12,2,32,1024]{3,2,1,0:T(8,128)(2,1)}, bf16[4,80,1024]{2,1,0:T(8,128)(2,1)}) custom-call(bf16[16,32,1024]{2,1,0:T(8,128)(2,1)} %bitcast.70, bf16[80,1024]{1,0:T(8,128)(2,1)} %fusion.29.refs_1_), custom_call_target="tpu_custom_call" | custom-call | tf_op jit(solution)/shard_map/send_last/pallas_call | solution.py:180
  559.1 1.6 broadcast_select_fusion
  560.7 2.1 convert.14
  562.8 0.9 fusion.45
  563.7 1.0 copy.46
  566.0 1.3 broadcast_select_fusion.1
  (77 shorter events, 5.4 us)
Async XLA Ops:
  0.6 15.6 %copy-start.5 = (bf16[1,3,1024,256]{3,2,1,0:T(8,128)(2,1)S(1)}, bf16[1,3,1024,256]{3,2,1,0:T(8,128)(2,1)}, u32[]{:S(2)}) copy-start(bf16[1,3,1024,256]{3,2,1,0:T(8,128)(2,1)} %param.17) | copy-start | bytes 4718596
  0.6 15.5 %copy-start.8 = (bf16[1,1024,256]{2,1,0:T(8,128)(2,1)S(1)}, bf16[1,1024,256]{2,1,0:T(8,128)(2,1)}, u32[]{:S(2)}) copy-start(bf16[1,1024,256]{2,1,0:T(8,128)(2,1)} %param.18) | copy-start | bytes 1572868
  14.7 3.1 copy-start.7
  16.2 1.5 copy-start.10
  16.2 1.7 copy-start.16
  16.2 1.8 copy-start.17
  16.2 1.8 copy-start.9
  18.9 260.4 %copy-start.4 = (bf16[6,2,64,1024]{3,2,1,0:T(8,128)(2,1)S(1)}, bf16[6,2,64,1024]{3,2,1,0:T(8,128)(2,1)}, u32[]{:S(2)}) copy-start(bf16[6,2,64,1024]{3,2,1,0:T(8,128)(2,1)} %param.14) | copy-start | bytes 4718596
  280.3 26.9 %copy-start = (f32[512,1024]{1,0:T(8,128)S(1)}, f32[512,1024]{1,0:T(8,128)}, u32[]{:S(2)}) copy-start(f32[512,1024]{1,0:T(8,128)} %get-tuple-element.89.refs_1_) | copy-start | bytes 6291460
  308.4 37.4 %copy-start.15 = (f32[4,2,2,512]{3,2,1,0:T(2,128)S(1)}, f32[4,2,2,512]{3,2,1,0:T(2,128)}, u32[]{:S(2)}) copy-start(f32[4,2,2,512]{3,2,1,0:T(2,128)} %get-tuple-element.98) | copy-start | bytes 98308
  349.4 51.8 %copy-start.14 = (f32[4,2,2,512]{3,2,1,0:T(2,128)S(1)}, f32[4,2,2,512]{3,2,1,0:T(2,128)}, u32[]{:S(2)}) copy-start(f32[4,2,2,512]{3,2,1,0:T(2,128)} %get-tuple-element.130) | copy-start | bytes 98308
  443.5 31.2 %copy-start.13 = (f32[4,2,2,512]{3,2,1,0:T(2,128)S(1)}, f32[4,2,2,512]{3,2,1,0:T(2,128)}, u32[]{:S(2)}) copy-start(f32[4,2,2,512]{3,2,1,0:T(2,128)} %get-tuple-element.136) | copy-start | bytes 98308
  475.4 53.7 %copy-start.6 = (bf16[12,2,32,1024]{3,2,1,0:T(8,128)(2,1)S(1)}, bf16[12,2,32,1024]{3,2,1,0:T(8,128)(2,1)}, u32[]{:S(2)}) copy-start(bf16[12,2,32,1024]{3,2,1,0:T(8,128)(2,1)} %get-tuple-element.142) | copy-start | bytes 4718596
  529.1 1.9 copy-start.11
  529.1 1.9 copy-start.12
  531.0 28.1 %copy-start.3 = (bf16[12,2,32,1024]{3,2,1,0:T(8,128)(2,1)S(1)}, bf16[12,2,32,1024]{3,2,1,0:T(8,128)(2,1)}, u32[]{:S(2)}) copy-start(bf16[12,2,32,1024]{3,2,1,0:T(8,128)(2,1)} %get-tuple-element.146) | copy-start | bytes 4718596
  560.7 2.1 copy-start.1
  563.7 2.3 copy-start.2

commit v3 on v2

--- a/solution.py
+++ b/solution.py
@@ -900,7 +900,7 @@
             stage3(i - LAG)
         if 0 <= i - 2 * LAG < count:
             stage4(i - 2 * LAG)
-        if i == 3:
+        if i == 6:
             send_tokens(1)
 
     def arrive_step(n):

time: 576 us -> 573 us (level)
  no operation moved by 1% of the time
where the time goes in v3:
time: 573 us; the launch traced here: 564 us
  Pallas kernels  534 us (93%)
  other arithmetic  16.7 us (3%)
  local copies, waits for them, and re-layouts  12.1 us (2%)
    pallas_call x1, Pallas kernels, forward_call(): pl.pallas_call(functools.partial(forward_kernel, plan, rows), grid=(plan[...  257 us
    pallas_call x3, Pallas kernels, attn_back(): pl.pallas_call(functools.partial(attn_back_kernel, causal, bool(cross), r...  146 us
    pallas_call x2, Pallas kernels, tail_back(): pl.pallas_call(functools.partial(tail_back_kernel, rider), grid=(groups *...  68.3 us
    pallas_call x1, Pallas kernels, tail_call(): pl.pallas_call(functools.partial(tail_kernel, rider), grid=(groups * (1 +...  27.3 us
    pallas_call x1, Pallas kernels, send_call(): pl.pallas_call(functools.partial(send_kernel, rider), in_specs=[anywhere]...  26.9 us

profile of v3, /device:TPU:0, one launch (start us, length us, event | category | flops | bytes accessed | tf_op | source)
XLA Modules:
  0.0 564.0 jit_solution(10072158007308413487)
XLA Ops:
  0.7 0.9 pad_add_fusion
  2.2 7.9 %ids.1 = s32[4,24,256]{2,1,0:T(8,128)} custom-call(s32[24,256]{1,0:T(8,128)} %reshape.727.ids), custom_call_target="tpu_custom_call" | custom-call | tf_op jit(solution)/shard_map/ids/pallas_call | solution.py:1298
  10.1 0.9 fusion.46
  11.9 0.7 fusion.43
  13.3 0.7 fusion.41
  14.7 0.7 stack.18.refs_7_
  15.4 0.8 fusion.25.refs_6_
  16.2 1.5 pad_maximum_fusion
  18.0 0.9 pad_maximum_fusion.1.refs_3_
  18.9 257.4 %forward.1 = (bf16[4,4096,256]{2,1,0:T(8,128)(2,1)}, bf16[4,1024,1024]{2,1,0:T(8,128)(2,1)}, bf16[4,1024,1024]{2,1,0:T(8,128)(2,1)}, bf16[4,1280,256]{2,1,0:T(8,...) custom-call(bf16[4096,256]{1,0:T(8,128)(2,1)} %bitcast.52, ...), custom_call_target="tpu_custom_call" | custom-call | tf_op jit(solution)/shard_map/forward/pallas_call | solution.py:1237
  276.4 1.0 slice_select_fusion.refs_4_
  277.3 27.3 %tail.1 = (bf16[4,512,1024]{2,1,0:T(8,128)(2,1)}, bf16[4,512,128]{2,1,0:T(8,128)(2,1)}, bf16[4,512,128]{2,1,0:T(8,128)(2,1)}, f32[512,1024]{1,0:T(8,128)}, f32[5...) custom-call(f32[512,1024]{1,0:T(8,128)} %get-tuple-element.77.refs_0_.refs_3_, ...), custom_call_target="tpu_custom_call" | custom-call | tf_op jit(solution)/shard_map/tail/pallas_call | solution.py:1385
  304.7 1.1 convert_element_type.56
  305.8 37.5 %tail_back.2 = (f32[512,1024]{1,0:T(8,128)}, bf16[4,512,256]{2,1,0:T(8,128)(2,1)}, bf16[4,4,32,1024]{3,2,1,0:T(8,128)(2,1)}, bf16[4,4,16,256]{3,2,1,0:T(8,128)(2,1)}, bf16[12,2,32,1024]{3,2,1,0:T(8,128)(2,1)}) custom-call(bf16[512,1024]{1,0:T(8,128)(2,1)} %bitcast.68, f32[512,1024]{1,0:T(8,128)} %get-tuple-element.82.refs_1_, ...), custom_call_target="tpu_custom_call" | custom-call | tf_op jit(solution)/shard_map/tail_back/pallas_call | solution.py:1544
  343.3 0.6 reshape.733.refs_7_
  344.0 1.2 fusion.22
  345.5 0.9 copy.43
  346.9 51.2 %attn_back.3 = (f32[512,1024]{1,0:T(8,128)}, bf16[4,512,256]{2,1,0:T(8,128)(2,1)}, f32[512,1024]{1,0:T(8,128)}, bf16[12,2,32,1024]{3,2,1,0:T(8,128)(2,1)}) custom-call(bf16[4,512,256]{2,1,0:T(8,128)(2,1)} %get-tuple-element.91.refs_0_, bf16[4,512,256]{2,1,0:T(8,128)(2,1)} %get-tuple-element.92.refs_1_, bf16[4,512,256]{2,1,0:T(8,128)(2,1)} %get-tuple-element.93.refs_2_, ...), custom_call_target="tpu_custom_call" | custom-call | tf_op jit(solution)/shard_map/attn_back/pallas_call | solution.py:1713
  398.2 0.6 reshape.736.refs_7_
  398.8 0.9 copy.44
  399.7 41.0 %attn_back.4 = (bf16[512,1024]{1,0:T(8,128)(2,1)}, bf16[12,2,32,1024]{3,2,1,0:T(8,128)(2,1)}, bf16[12,2,16,256]{3,2,1,0:T(8,128)(2,1)}) custom-call(bf16[4,512,256]{2,1,0:T(8,128)(2,1)} %get-tuple-element.123.refs_0_, bf16[4,512,256]{2,1,0:T(8,128)(2,1)} %get-tuple-element.124.refs_1_, bf16[4,512,256]{2,1,0:T(8,128)(2,1)} %get-tuple-element.125.refs_2_, ...), custom_call_target="tpu_custom_call" | custom-call | tf_op jit(solution)/shard_map/attn_back/pallas_call | solution.py:1713
  440.8 30.9 %tail_back.3 = (f32[512,1024]{1,0:T(8,128)}, bf16[4,512,256]{2,1,0:T(8,128)(2,1)}, bf16[4,4,32,1024]{3,2,1,0:T(8,128)(2,1)}, bf16[4,4,16,256]{3,2,1,0:T(8,128)(2,1)}, bf16[12,2,32,1024]{3,2,1,0:T(8,128)(2,1)}) custom-call(f32[512,1024]{1,0:T(8,128)} %get-tuple-element.112.refs_0_, f32[512,1024]{1,0:T(8,128)} %get-tuple-element.89.refs_1_, ...), custom_call_target="tpu_custom_call" | custom-call | tf_op jit(solution)/shard_map/tail_back/pallas_call | solution.py:1544
  471.6 0.6 reshape.740.refs_7_
  472.3 53.7 %attn_back.5 = (bf16[512,1024]{1,0:T(8,128)(2,1)}, bf16[12,2,32,1024]{3,2,1,0:T(8,128)(2,1)}, bf16[12,2,16,256]{3,2,1,0:T(8,128)(2,1)}) custom-call(bf16[4,512,256]{2,1,0:T(8,128)(2,1)} %get-tuple-element.106.refs_0_, bf16[4,512,256]{2,1,0:T(8,128)(2,1)} %get-tuple-element.107.refs_1_, bf16[4,512,256]{2,1,0:T(8,128)(2,1)} %get-tuple-element.108.refs_2_, ...), custom_call_target="tpu_custom_call" | custom-call | tf_op jit(solution)/shard_map/attn_back/pallas_call | solution.py:1713
  526.0 1.9 select_reduce_fusion
  528.0 0.7 fusion.29.refs_1_
  528.7 26.9 %send_last.1 = (bf16[12,2,32,1024]{3,2,1,0:T(8,128)(2,1)}, bf16[4,80,1024]{2,1,0:T(8,128)(2,1)}) custom-call(bf16[16,32,1024]{2,1,0:T(8,128)(2,1)} %bitcast.70, bf16[80,1024]{1,0:T(8,128)(2,1)} %fusion.29.refs_1_), custom_call_target="tpu_custom_call" | custom-call | tf_op jit(solution)/shard_map/send_last/pallas_call | solution.py:180
  555.6 1.6 broadcast_select_fusion
  557.2 2.1 convert.14
  559.4 0.9 fusion.45
  560.3 1.0 copy.46
  562.5 1.3 broadcast_select_fusion.1
  (77 shorter events, 5.4 us)
Async XLA Ops:
  0.6 15.6 %copy-start.5 = (bf16[1,3,1024,256]{3,2,1,0:T(8,128)(2,1)S(1)}, bf16[1,3,1024,256]{3,2,1,0:T(8,128)(2,1)}, u32[]{:S(2)}) copy-start(bf16[1,3,1024,256]{3,2,1,0:T(8,128)(2,1)} %param.17) | copy-start | bytes 4718596
  0.6 15.5 %copy-start.8 = (bf16[1,1024,256]{2,1,0:T(8,128)(2,1)S(1)}, bf16[1,1024,256]{2,1,0:T(8,128)(2,1)}, u32[]{:S(2)}) copy-start(bf16[1,1024,256]{2,1,0:T(8,128)(2,1)} %param.18) | copy-start | bytes 1572868
  14.7 3.1 copy-start.7
  16.2 1.5 copy-start.10
  16.2 1.7 copy-start.16
  16.2 1.8 copy-start.17
  16.2 1.8 copy-start.9
  18.9 257.4 %copy-start.4 = (bf16[6,2,64,1024]{3,2,1,0:T(8,128)(2,1)S(1)}, bf16[6,2,64,1024]{3,2,1,0:T(8,128)(2,1)}, u32[]{:S(2)}) copy-start(bf16[6,2,64,1024]{3,2,1,0:T(8,128)(2,1)} %param.14) | copy-start | bytes 4718596
  277.3 27.3 %copy-start = (f32[512,1024]{1,0:T(8,128)S(1)}, f32[512,1024]{1,0:T(8,128)}, u32[]{:S(2)}) copy-start(f32[512,1024]{1,0:T(8,128)} %get-tuple-element.89.refs_1_) | copy-start | bytes 6291460
  305.8 37.5 %copy-start.15 = (f32[4,2,2,512]{3,2,1,0:T(2,128)S(1)}, f32[4,2,2,512]{3,2,1,0:T(2,128)}, u32[]{:S(2)}) copy-start(f32[4,2,2,512]{3,2,1,0:T(2,128)} %get-tuple-element.98) | copy-start | bytes 98308
  346.9 51.3 %copy-start.14 = (f32[4,2,2,512]{3,2,1,0:T(2,128)S(1)}, f32[4,2,2,512]{3,2,1,0:T(2,128)}, u32[]{:S(2)}) copy-start(f32[4,2,2,512]{3,2,1,0:T(2,128)} %get-tuple-element.130) | copy-start | bytes 98308
  440.8 30.9 %copy-start.13 = (f32[4,2,2,512]{3,2,1,0:T(2,128)S(1)}, f32[4,2,2,512]{3,2,1,0:T(2,128)}, u32[]{:S(2)}) copy-start(f32[4,2,2,512]{3,2,1,0:T(2,128)} %get-tuple-element.136) | copy-start | bytes 98308
  472.3 53.7 %copy-start.6 = (bf16[12,2,32,1024]{3,2,1,0:T(8,128)(2,1)S(1)}, bf16[12,2,32,1024]{3,2,1,0:T(8,128)(2,1)}, u32[]{:S(2)}) copy-start(bf16[12,2,32,1024]{3,2,1,0:T(8,128)(2,1)} %get-tuple-element.142) | copy-start | bytes 4718596
  526.0 1.9 copy-start.11
  526.0 1.9 copy-start.12
  527.9 27.7 %copy-start.3 = (bf16[12,2,32,1024]{3,2,1,0:T(8,128)(2,1)S(1)}, bf16[12,2,32,1024]{3,2,1,0:T(8,128)(2,1)}, u32[]{:S(2)}) copy-start(bf16[12,2,32,1024]{3,2,1,0:T(8,128)(2,1)} %get-tuple-element.146) | copy-start | bytes 4718596
  557.2 2.1 copy-start.1
  560.3 2.3 copy-start.2

commit v4 on v3

--- a/solution.py
+++ b/solution.py
@@ -64,7 +64,7 @@
             )
             for a, k in arrays
         ]
-        count = len(arrays)
+        count = max(len(arrays), 1)
         self.scratch = [
             pltpu.SemaphoreType.DMA((count, 16)),
             pltpu.SemaphoreType.DMA((count, 16, 2)),
@@ -1941,7 +1941,7 @@
         def pieces(parts):
             return [v.reshape((chips,) + v.shape[2:]) for v in parts]
 
-        (grad_cross, do), dec_parts, (out_enc,) = tail_back(
+        (grad_cross, do), dec_parts, _ = tail_back(
             cotangent,
             dec_y,
             dec_yr,
@@ -1953,13 +1953,13 @@
             dec_a,
             dec_w[4],
             1,
-            scatter([(tokens(encoded_bf), 0)], 2),
-        )
-        (dpre, do, grad_encoded), (out_dec,) = attn_back(
+            scatter([], 2),
+        )
+        (dpre, do, grad_encoded), (out_enc, out_dec) = attn_back(
             heads(CQ, MK, MKX, MV, MVX, CO, CL, do),
             [feats[3], feats[1], feats[2], *cross_ids[1]],
             False,
-            scatter([(tokens(decoded), 1)], 3),
+            scatter([(tokens(encoded_bf), 0), (tokens(decoded), 1)], 3),
             grad_cross,
             (dec_w[4], enc_w[4]),
             (kept[DH], kept[DR], dec_w[0]),

time: 573 us -> 571 us (level)
    pallas_call x2, Pallas kernels: 68.3 us -> 56.7 us  [tail_back(): pl.pallas_call(functools.partial(tail_back_kernel, rider), grid=(groups *...]
    pallas_call x3, Pallas kernels: 146 us -> 155 us  [attn_back(): pl.pallas_call(functools.partial(attn_back_kernel, causal, bool(cross), r...]
where the time goes in v4:
time: 571 us; the launch traced here: 562 us
  Pallas kernels  532 us (93%)
  other arithmetic  16.7 us (3%)
  local copies, waits for them, and re-layouts  12.2 us (2%)
    pallas_call x1, Pallas kernels, forward_call(): pl.pallas_call(functools.partial(forward_kernel, plan, rows), grid=(plan[...  257 us
    pallas_call x3, Pallas kernels, attn_back(): pl.pallas_call(functools.partial(attn_back_kernel, causal, bool(cross), r...  155 us
    pallas_call x2, Pallas kernels, tail_back(): pl.pallas_call(functools.partial(tail_back_kernel, rider), grid=(groups *...  56.7 us
    pallas_call x1, Pallas kernels, tail_call(): pl.pallas_call(functools.partial(tail_kernel, rider), grid=(groups * (1 +...  27.2 us
    pallas_call x1, Pallas kernels, send_call(): pl.pallas_call(functools.partial(send_kernel, rider), in_specs=[anywhere]...  27.2 us

profile of v4, /device:TPU:0, one launch (start us, length us, event | category | flops | bytes accessed | tf_op | source)
XLA Modules:
  0.0 561.7 jit_solution(9481184783605691423)
XLA Ops:
  0.7 0.9 pad_add_fusion
  2.2 7.9 %ids.1 = s32[4,24,256]{2,1,0:T(8,128)} custom-call(s32[24,256]{1,0:T(8,128)} %reshape.727.ids), custom_call_target="tpu_custom_call" | custom-call | tf_op jit(solution)/shard_map/ids/pallas_call | solution.py:1298
  10.1 0.9 fusion.46
  11.9 0.7 fusion.43
  13.3 0.7 fusion.41
  14.7 0.7 stack.18.refs_7_
  15.4 0.8 fusion.25.refs_6_
  16.2 1.5 pad_maximum_fusion
  18.0 0.9 pad_maximum_fusion.1.refs_3_
  18.9 257.4 %forward.1 = (bf16[4,4096,256]{2,1,0:T(8,128)(2,1)}, bf16[4,1024,1024]{2,1,0:T(8,128)(2,1)}, bf16[4,1024,1024]{2,1,0:T(8,128)(2,1)}, bf16[4,1280,256]{2,1,0:T(8,...) custom-call(bf16[4096,256]{1,0:T(8,128)(2,1)} %bitcast.52, ...), custom_call_target="tpu_custom_call" | custom-call | tf_op jit(solution)/shard_map/forward/pallas_call | solution.py:1237
  276.4 1.0 slice_select_fusion.refs_4_
  277.3 27.2 %tail.1 = (bf16[4,512,1024]{2,1,0:T(8,128)(2,1)}, bf16[4,512,128]{2,1,0:T(8,128)(2,1)}, bf16[4,512,128]{2,1,0:T(8,128)(2,1)}, f32[512,1024]{1,0:T(8,128)}, f32[5...) custom-call(f32[512,1024]{1,0:T(8,128)} %get-tuple-element.83.refs_0_.refs_3_, ...), custom_call_target="tpu_custom_call" | custom-call | tf_op jit(solution)/shard_map/tail/pallas_call | solution.py:1385
  304.5 28.4 %tail_back.2 = (f32[512,1024]{1,0:T(8,128)}, bf16[4,512,256]{2,1,0:T(8,128)(2,1)}, bf16[4,4,32,1024]{3,2,1,0:T(8,128)(2,1)}, bf16[4,4,16,256]{3,2,1,0:T(8,128)(2,1)}) custom-call(bf16[512,1024]{1,0:T(8,128)(2,1)} %bitcast.68, f32[512,1024]{1,0:T(8,128)} %get-tuple-element.88.refs_1_, f32[512,128]{1,0:T(8,128)} %get-tuple-element.89.refs_2_, ...), custom_call_target="tpu_custom_call" | custom-call | tf_op jit(solution)/shard_map/tail_back/pallas_call | solution.py:1544
  333.0 1.1 convert_element_type.59
  334.1 0.6 reshape.732.refs_7_
  334.7 1.2 fusion.22
  336.3 0.9 copy.43
  337.7 51.2 %attn_back.3 = (f32[512,1024]{1,0:T(8,128)}, bf16[4,512,256]{2,1,0:T(8,128)(2,1)}, f32[512,1024]{1,0:T(8,128)}, bf16[12,2,32,1024]{3,2,1,0:T(8,128)(2,1)}, bf16[12,2,32,1024]{3,2,1,0:T(8,128)(2,1)}) custom-call(bf16[4,512,256]{2,1,0:T(8,128)(2,1)} %get-tuple-element.77.refs_0_, bf16[4,512,256]{2,1,0:T(8,128)(2,1)} %get-tuple-element.78.refs_1_, ...), custom_call_target="tpu_custom_call" | custom-call | tf_op jit(solution)/shard_map/attn_back/pallas_call | solution.py:1713
  388.9 0.6 reshape.736.refs_7_
  389.6 0.9 copy.44
  390.4 49.3 %attn_back.4 = (bf16[512,1024]{1,0:T(8,128)(2,1)}, bf16[12,2,32,1024]{3,2,1,0:T(8,128)(2,1)}, bf16[12,2,16,256]{3,2,1,0:T(8,128)(2,1)}) custom-call(bf16[4,512,256]{2,1,0:T(8,128)(2,1)} %get-tuple-element.123.refs_0_, bf16[4,512,256]{2,1,0:T(8,128)(2,1)} %get-tuple-element.124.refs_1_, bf16[4,512,256]{2,1,0:T(8,128)(2,1)} %get-tuple-element.125.refs_2_, ...), custom_call_target="tpu_custom_call" | custom-call | tf_op jit(solution)/shard_map/attn_back/pallas_call | solution.py:1713
  439.7 28.3 %tail_back.3 = (f32[512,1024]{1,0:T(8,128)}, bf16[4,512,256]{2,1,0:T(8,128)(2,1)}, bf16[4,4,32,1024]{3,2,1,0:T(8,128)(2,1)}, bf16[4,4,16,256]{3,2,1,0:T(8,128)(2,1)}, bf16[12,2,32,1024]{3,2,1,0:T(8,128)(2,1)}) custom-call(f32[512,1024]{1,0:T(8,128)} %get-tuple-element.112.refs_0_, f32[512,1024]{1,0:T(8,128)} %get-tuple-element.102.refs_1_, ...), custom_call_target="tpu_custom_call" | custom-call | tf_op jit(solution)/shard_map/tail_back/pallas_call | solution.py:1544
  468.1 0.6 reshape.740.refs_7_
  468.7 54.6 %attn_back.5 = (bf16[512,1024]{1,0:T(8,128)(2,1)}, bf16[12,2,32,1024]{3,2,1,0:T(8,128)(2,1)}, bf16[12,2,16,256]{3,2,1,0:T(8,128)(2,1)}) custom-call(bf16[4,512,256]{2,1,0:T(8,128)(2,1)} %get-tuple-element.106.refs_0_, bf16[4,512,256]{2,1,0:T(8,128)(2,1)} %get-tuple-element.107.refs_1_, bf16[4,512,256]{2,1,0:T(8,128)(2,1)} %get-tuple-element.108.refs_2_, ...), custom_call_target="tpu_custom_call" | custom-call | tf_op jit(solution)/shard_map/attn_back/pallas_call | solution.py:1713
  523.4 1.9 select_reduce_fusion
  525.4 0.7 fusion.29.refs_1_
  526.0 27.2 %send_last.1 = (bf16[12,2,32,1024]{3,2,1,0:T(8,128)(2,1)}, bf16[4,80,1024]{2,1,0:T(8,128)(2,1)}) custom-call(bf16[16,32,1024]{2,1,0:T(8,128)(2,1)} %bitcast.70, bf16[80,1024]{1,0:T(8,128)(2,1)} %fusion.29.refs_1_), custom_call_target="tpu_custom_call" | custom-call | tf_op jit(solution)/shard_map/send_last/pallas_call | solution.py:180
  553.2 1.6 broadcast_select_fusion
  554.8 2.1 convert.14
  557.0 0.9 fusion.45
  557.9 1.0 copy.46
  560.2 1.3 broadcast_select_fusion.1
  (77 shorter events, 5.4 us)
Async XLA Ops:
  0.6 15.6 %copy-start.5 = (bf16[1,3,1024,256]{3,2,1,0:T(8,128)(2,1)S(1)}, bf16[1,3,1024,256]{3,2,1,0:T(8,128)(2,1)}, u32[]{:S(2)}) copy-start(bf16[1,3,1024,256]{3,2,1,0:T(8,128)(2,1)} %param.17) | copy-start | bytes 4718596
  0.6 15.5 %copy-start.8 = (bf16[1,1024,256]{2,1,0:T(8,128)(2,1)S(1)}, bf16[1,1024,256]{2,1,0:T(8,128)(2,1)}, u32[]{:S(2)}) copy-start(bf16[1,1024,256]{2,1,0:T(8,128)(2,1)} %param.18) | copy-start | bytes 1572868
  14.7 3.1 copy-start.7
  16.2 1.5 copy-start.10
  16.2 1.7 copy-start.16
  16.2 1.8 copy-start.17
  16.2 1.8 copy-start.9
  18.9 257.4 %copy-start.4 = (bf16[6,2,64,1024]{3,2,1,0:T(8,128)(2,1)S(1)}, bf16[6,2,64,1024]{3,2,1,0:T(8,128)(2,1)}, u32[]{:S(2)}) copy-start(bf16[6,2,64,1024]{3,2,1,0:T(8,128)(2,1)} %param.14) | copy-start | bytes 4718596
  304.5 28.4 %copy-start = (f32[512,1024]{1,0:T(8,128)S(1)}, f32[512,1024]{1,0:T(8,128)}, u32[]{:S(2)}) copy-start(f32[512,1024]{1,0:T(8,128)} %get-tuple-element.102.refs_1_) | copy-start | bytes 6291460
  332.9 1.1 copy-start.15
  337.7 51.2 %copy-start.14 = (f32[4,2,2,512]{3,2,1,0:T(2,128)S(1)}, f32[4,2,2,512]{3,2,1,0:T(2,128)}, u32[]{:S(2)}) copy-start(f32[4,2,2,512]{3,2,1,0:T(2,128)} %get-tuple-element.130) | copy-start | bytes 98308
  439.7 28.3 %copy-start.13 = (f32[4,2,2,512]{3,2,1,0:T(2,128)S(1)}, f32[4,2,2,512]{3,2,1,0:T(2,128)}, u32[]{:S(2)}) copy-start(f32[4,2,2,512]{3,2,1,0:T(2,128)} %get-tuple-element.136) | copy-start | bytes 98308
  468.7 54.6 %copy-start.6 = (bf16[12,2,32,1024]{3,2,1,0:T(8,128)(2,1)S(1)}, bf16[12,2,32,1024]{3,2,1,0:T(8,128)(2,1)}, u32[]{:S(2)}) copy-start(bf16[12,2,32,1024]{3,2,1,0:T(8,128)(2,1)} %get-tuple-element.142) | copy-start | bytes 4718596
  523.4 1.9 copy-start.11
  523.4 1.9 copy-start.12
  525.3 28.0 %copy-start.3 = (bf16[12,2,32,1024]{3,2,1,0:T(8,128)(2,1)S(1)}, bf16[12,2,32,1024]{3,2,1,0:T(8,128)(2,1)}, u32[]{:S(2)}) copy-start(bf16[12,2,32,1024]{3,2,1,0:T(8,128)(2,1)} %get-tuple-element.146) | copy-start | bytes 4718596
  554.8 2.1 copy-start.1
  557.9 2.3 copy-start.2
